TPU v7x, 512 devices: a whole 4x8x8 slice. The times are simulated.
512 devices in a mesh: seq: 128 (over z, y, core), pack: 4 (over x).
Axes of the slice: x: 4, y: 8, z: 8, core: 2. Of those that a mesh axis runs over, the one named last changes fastest.
Arguments:
- queries: bfloat16 [131072, 2048], P(('pack', 'seq')), parts along dimension 0, may hold values from -10 to 10
- keys: bfloat16 [131072, 512], P(('pack', 'seq')), parts along dimension 0, may hold values from -10 to 10
- values: bfloat16 [131072, 512], P(('pack', 'seq')), parts along dimension 0, may hold values from -6 to 6
- lengths: int32 [512], P('pack'), parts along dimension 0, may hold values from 1 to 4096, 32768 in all
- home: int32 [1024], P('pack'), parts along dimension 0, may hold values from 0 to 127, as said below
Outputs:
- attended: bfloat16 [131072, 2048], P(('pack', 'seq')), parts along dimension 0
There are 4 independent parts, one for each index of `pack`. A program takes and returns all parts, laid end to end along the dimension named above; each array names one. Nothing has to cross between parts.
Inputs may be any that keep to these rules, and one draw needn't show every extreme that they name: Block b covers positions b * 128 to b * 128 + 127. home[b] is 2 * (b // 4) or that plus one, and every device index is home of exactly 2 blocks.
All inputs are finite; a program needn't handle non-finite values.
Results may differ from a plain program's by a relative error of at most 0.0033.
Values may be sent and summed in bfloat16 or wider, within the bound.
No kernel may reach another device: no remote copies, remote signals or barrier semaphores. Data moves between devices by JAX's collectives and lax.ppermute only.
A program may use at most 64 MiB of HBM per device.

v0:
```python
import functools
import math

import jax
import jax.numpy as jnp
from jax import lax
from jax.experimental import pallas as pl
from jax.experimental.pallas import tpu as pltpu
from jax.sharding import PartitionSpec as P

HD = 128
BLOCK = 128
WINDOW = 2048
ROWS = 256
HEADS = 8
GROUP = 4
HALF = HEADS * HD
KVW = 512
FACTOR = HD**-0.5 * math.log2(math.e)
NEG = -1e30
PLAN = 20.0
VLIM = 24 * 1024 * 1024
VSPEC = pl.BlockSpec(memory_space=pltpu.VMEM)
SSPEC = pl.BlockSpec(memory_space=pltpu.SMEM)
ASPEC = pl.BlockSpec(memory_space=pl.ANY)
STATE = [pltpu.VMEM((2 * ROWS, HALF), jnp.float32)] * 3
TOKEN = [pltpu.VMEM((8, 128), jnp.float32)]
POS, LOW_FIRST, LOW_LAST, MINE, SLOT = 1, 5, 9, 13, 17


def params(limit=VLIM):
    return pltpu.CompilerParams(vmem_limit_bytes=limit)


def cost(micros):
    return pl.CostEstimate(
        flops=int(micros * 1.15e9), bytes_accessed=1 << 20, transcendentals=1 << 20
    )


def fast(x):
    return pltpu.with_memory_space_constraint(x, pltpu.VMEM)


def touch(buffer, token):
    return pl.pallas_call(
        lambda buffer_ref, token_ref, out_ref: None,
        out_shape=pltpu.VMEM(buffer.shape, buffer.dtype),
        in_specs=[ASPEC, ASPEC],
        out_specs=ASPEC,
        input_output_aliases={0: 0},
        compiler_params=params(1024 * 1024),
        name="touch",
    )(fast(buffer), fast(token))


def near_kernel(k, v, near, sems):
    core = lax.rem(lax.axis_index("seq"), 2)
    cols = pl.ds(pl.multiple_of(core * 256, 256), 256)
    copies = [
        pltpu.make_async_copy(source.at[:, cols], near.at[:, i * 256 : i * 256 + 256], sems.at[i])
        for i, source in enumerate((k, v))
    ]
    for copy in copies:
        copy.start()
    for copy in copies:
        copy.wait()


def pack_kernel(q, k, v, near, cross, swap, own, sems):
    core = lax.rem(lax.axis_index("seq"), 2)
    other = 1 - core

    def cols(index, width):
        return pl.ds(pl.multiple_of(index * width, width), width)

    moves = [
        (k.at[:, cols(other, 256)], cross.at[:, 0:256]),
        (v.at[:, cols(other, 256)], cross.at[:, 256:512]),
        (q.at[:, cols(other, HALF)], swap.at[:, 0:HALF]),
        (k.at[:, cols(other, 256)], swap.at[:, HALF : HALF + 256]),
        (v.at[:, cols(other, 256)], swap.at[:, HALF + 256 : HALF + 512]),
        (q.at[:, cols(core, HALF)], own),
    ]
    copies = [
        pltpu.make_async_copy(source, target, sems.at[i])
        for i, (source, target) in enumerate(moves)
    ]
    for copy in copies:
        copy.start()
    for copy in copies:
        copy.wait()


def plan_kernel(lengths, home, meta, low_key):
    device = lax.axis_index("seq")
    core = lax.rem(device, 2)
    docs = lengths.shape[1]
    wide = jnp.broadcast_to(lengths[...].astype(jnp.float32), (docs, docs))
    before = lax.broadcasted_iota(jnp.int32, (docs, docs), 0) < lax.broadcasted_iota(
        jnp.int32, (docs, docs), 1
    )
    starts = jnp.sum(jnp.where(before, wide.T, jnp.float32(0.0)), axis=0, keepdims=True)
    meta[0] = core
    for block in range(4):
        half = device if block < 2 else device + 1 - 2 * core
        pos = half * ROWS + (block % 2) * BLOCK
        meta[POS + block] = pos
        for slot, shift in ((LOW_FIRST, 0), (LOW_LAST, BLOCK - 1)):
            at = (pos + shift).astype(jnp.float32)
            first = jnp.max(jnp.where(starts <= at, starts, jnp.float32(0.0)))
            meta[slot + block] = jnp.maximum(
                first.astype(jnp.int32), pos + shift - (WINDOW - 1)
            )
        rows = (pos + lax.broadcasted_iota(jnp.int32, (BLOCK, docs), 0)).astype(jnp.float32)
        first = jnp.max(
            jnp.where(starts <= rows, starts, jnp.float32(0.0)), axis=1, keepdims=True
        )
        low_key[pl.ds(block * BLOCK, BLOCK), :] = jnp.maximum(
            jnp.broadcast_to(first, (BLOCK, docs)), rows - (WINDOW - 1)
        ).astype(jnp.int32)
    homes = [home[(device - core) * 2 + t] for t in range(4)]
    for t in range(4):
        rank = jnp.int32(0)
        for u in range(t):
            rank = rank + (homes[u] == homes[t]).astype(jnp.int32)
        place = lax.rem(t + 2 * core, 4)
        meta[MINE + place] = (homes[t] == device).astype(jnp.int32)
        meta[SLOT + place] = rank


def row_span(row):
    return pl.ds(row if isinstance(row, int) else pl.multiple_of(row, BLOCK), BLOCK)


def stacked(ref, rows, kvh):
    return jnp.concatenate(
        [ref[rows, pl.ds((kvh * GROUP + g) * HD, HD)] for g in range(GROUP)], axis=0
    )


def fold(q, kv, kv_row, state, row, bias=None, first=False, span=ROWS):
    acc, top, low = state
    rows = row_span(row)
    key_rows = pl.ds(kv_row, span)
    for kvh in range(HEADS // GROUP):
        keys = kv[key_rows, kvh * HD : (kvh + 1) * HD]
        vals = kv[key_rows, 256 + kvh * HD : 256 + (kvh + 1) * HD]
        scores = (
            lax.dot_general(
                stacked(q, rows, kvh),
                keys,
                (((1,), (1,)), ((), ())),
                preferred_element_type=jnp.float32,
            )
            * FACTOR
        )
        if bias is not None:
            scores = scores + jnp.concatenate([bias] * GROUP, axis=0)
        peak = jnp.max(scores, axis=1, keepdims=True)
        if first:
            new = jnp.broadcast_to(peak, (GROUP * BLOCK, HD))
        else:
            old = stacked(top, rows, kvh)
            new = jnp.maximum(old, peak)
            keep = jnp.exp2(old - new)
        weights = jnp.exp2(scores - jnp.concatenate([new] * (span // HD), axis=1))
        mixed = jnp.dot(weights.astype(jnp.bfloat16), vals, preferred_element_type=jnp.float32)
        part = weights[:, :HD]
        if span > HD:
            part = part + weights[:, HD:]
        for g in range(GROUP):
            cols = pl.ds((kvh * GROUP + g) * HD, HD)
            cut = slice(g * BLOCK, (g + 1) * BLOCK)
            top[rows, cols] = new[cut]
            if first:
                low[rows, cols] = part[cut]
                acc[rows, cols] = mixed[cut]
            else:
                low[rows, cols] = low[rows, cols] * keep[cut] + part[cut]
                acc[rows, cols] = acc[rows, cols] * keep[cut] + mixed[cut]


def bias_of(meta, low_key, block, key_base, span=ROWS):
    last = meta[POS + block] + lax.broadcasted_iota(jnp.int32, (BLOCK, HD), 0)
    least = low_key[row_span(block * BLOCK), :]
    parts = []
    for start in range(0, span, HD):
        key = key_base + start + lax.broadcasted_iota(jnp.int32, (BLOCK, HD), 1)
        allowed = (key <= last) & (key >= least)
        parts.append(jnp.where(allowed, jnp.float32(0.0), jnp.float32(NEG)))
    return jnp.concatenate(parts, axis=1)


def half_update(meta, low_key, q, kv, kv_row, half, key_base, state):
    block = half * 2
    last_key = key_base + ROWS - 1
    some = (key_base <= meta[POS + block + 1] + BLOCK - 1) & (last_key >= meta[LOW_FIRST + block])
    full = (last_key <= meta[POS + block]) & (key_base >= meta[LOW_LAST + block + 1])

    @pl.when(full)
    def _():
        for step in range(2):
            fold(q, kv, kv_row, state, (block + step) * BLOCK)

    @pl.when(some & jnp.logical_not(full))
    def _():
        for step in range(2):
            bias = bias_of(meta, low_key, block + step, key_base)
            fold(q, kv, kv_row, state, (block + step) * BLOCK, bias)


def first_kernel(meta, low_key, own, near, recv, q, acc, top, low, token, kv):
    state = (acc, top, low)
    q[0:ROWS, :] = own[...]
    q[ROWS : 2 * ROWS, :] = recv[:, 0:HALF]
    kv[0:ROWS, :] = near[...]
    kv[ROWS : 2 * ROWS, :] = recv[:, HALF : HALF + KVW]

    def body(half, carry):
        kv_row = pl.multiple_of(half * ROWS, ROWS)
        base = meta[POS + half * 2]
        for step in range(2):
            span = (step + 1) * BLOCK
            block = half * 2 + step
            bias = bias_of(meta, low_key, block, base, span)
            fold(q, kv, kv_row, state, block * BLOCK, bias, True, span)
        return carry

    lax.fori_loop(0, 2, body, 0)
    late = 1 - meta[0]
    early_row = pl.multiple_of((1 - late) * ROWS, ROWS)
    half_update(meta, low_key, q, kv, early_row, late, meta[POS + 2 - late * 2], state)


def next_kernel(back, side, meta, low_key, q, kv, *refs):
    state = refs[3:6]
    base = meta[POS + side * 2] - back * 2 * ROWS

    def body(half, carry):
        half_update(meta, low_key, q, kv, 0, half, base, state)
        return carry

    lax.fori_loop(0, 2, body, 0)


def last_kernel(back, side, meta, low_key, q, kv, a, t, d, keep, send, acc, top, low):
    next_kernel(back, side, meta, low_key, q, kv, a, t, d, acc, top, low)

    def body(block, carry):
        rows = row_span(block * BLOCK)
        slot = pl.ds(pl.multiple_of(meta[SLOT + block] * BLOCK, BLOCK), BLOCK)

        def write(ref, rows=rows, slot=slot):
            for head in range(HEADS):
                cols = pl.ds(head * HD, HD)
                total = jnp.sum(low[rows, cols], axis=1, keepdims=True)
                ref[slot, cols] = (acc[rows, cols] / total).astype(jnp.bfloat16)

        @pl.when(meta[MINE + block] == 1)
        def _(write=write):
            write(keep)

        @pl.when(meta[MINE + block] == 0)
        def _(write=write):
            write(send)

        return carry

    lax.fori_loop(0, 4, body, 0)


def join_kernel(keep, got, out, sems):
    core = lax.rem(lax.axis_index("seq"), 2)
    copies = []
    for i, (source, half) in enumerate(((keep, core), (got, 1 - core))):
        cols = pl.ds(pl.multiple_of(half * HALF, HALF), HALF)
        copies.append(pltpu.make_async_copy(source, out.at[:, cols], sems.at[i]))
    for copy in copies:
        copy.start()
    for copy in copies:
        copy.wait()


def local(queries, keys, values, lengths, home):
    count = lax.axis_size("seq")
    bf16 = jnp.bfloat16
    hbm = pl.BlockSpec(memory_space=pltpu.HBM)
    near = pl.pallas_call(
        near_kernel,
        out_shape=pltpu.VMEM((ROWS, KVW), bf16),
        in_specs=[hbm] * 2,
        out_specs=VSPEC,
        scratch_shapes=[pltpu.SemaphoreType.DMA((2,))],
        compiler_params=params(60 * 1024 * 1024),
        name="near",
    )(keys, values)
    cross, swap, own = pl.pallas_call(
        pack_kernel,
        out_shape=[
            pltpu.VMEM((ROWS, KVW), bf16),
            pltpu.VMEM((ROWS, HALF + KVW), bf16),
            pltpu.VMEM((ROWS, HALF), bf16),
        ],
        in_specs=[hbm] * 3 + [ASPEC],
        out_specs=[VSPEC] * 3,
        scratch_shapes=[pltpu.SemaphoreType.DMA((6,))],
        compiler_params=params(60 * 1024 * 1024),
        name="pack",
    )(queries, keys, values, fast(near))

    same = [(i, i + 2) for i in range(count - 2)]
    other = [(i, (i ^ 1) + 2) for i in range(count - 2)]
    pair = [(i, i ^ 1) for i in range(count)]
    shift = functools.partial(lax.ppermute, axis_name="seq")
    arrived = [shift(near, perm=same), shift(cross, perm=other)]
    recv = fast(shift(swap, perm=pair))

    meta, low_key = pl.pallas_call(
        plan_kernel,
        out_shape=[pltpu.SMEM((32,), jnp.int32), pltpu.VMEM((2 * ROWS, HD), jnp.int32)],
        in_specs=[VSPEC, SSPEC],
        out_specs=[SSPEC, VSPEC],
        compiler_params=params(),
        cost_estimate=cost(PLAN),
        name="plan",
    )(lengths[None, :], home)
    meta = pltpu.with_memory_space_constraint(meta, pltpu.SMEM)
    low_key, own = fast(low_key), fast(own)

    q, *state, token = pl.pallas_call(
        first_kernel,
        out_shape=[pltpu.VMEM((2 * ROWS, HALF), bf16)] + STATE + TOKEN,
        in_specs=[SSPEC] + [VSPEC] * 4,
        out_specs=[VSPEC] * 4 + [ASPEC],
        scratch_shapes=[pltpu.VMEM((2 * ROWS, KVW), bf16)],
        compiler_params=params(),
        cost_estimate=cost(3.0),
        name="first",
    )(meta, low_key, own, fast(near), recv)
    tokens = [None, token]
    for index in range(6):
        kv = arrived[index]
        if index:
            kv = arrived[index] = touch(kv, tokens[index])
        arrived.append(shift(kv, perm=same))
        if index == 0:
            continue
        state, token = step(index - 1, arrived, meta, low_key, q, state)
        tokens.append(token)
    for index in (5, 6):
        state, token = step(index, arrived, meta, low_key, q, state)
    keep, send = step(7, arrived, meta, low_key, q, state)
    got = shift(send, perm=pair)
    return pl.pallas_call(
        join_kernel,
        out_shape=jax.ShapeDtypeStruct((ROWS, 2 * HALF), bf16),
        in_specs=[VSPEC] * 2,
        out_specs=pl.BlockSpec(memory_space=pltpu.HBM),
        scratch_shapes=[pltpu.SemaphoreType.DMA((2,))],
        compiler_params=params(),
        name="join",
    )(fast(keep), fast(got))


def step(index, arrived, meta, low_key, q, state):
    last = index == 7
    kernel = last_kernel if last else next_kernel
    extra = [pltpu.VMEM((ROWS, HALF), jnp.bfloat16)] * 2 if last else []
    results = pl.pallas_call(
        functools.partial(kernel, index // 2 + 1, index % 2),
        out_shape=extra + STATE + ([] if last else TOKEN),
        in_specs=[SSPEC] + [VSPEC] * 6,
        out_specs=[VSPEC] * (len(extra) + 3) + ([] if last else [ASPEC]),
        input_output_aliases={4 + i: len(extra) + i for i in range(3)},
        compiler_params=params(),
        cost_estimate=cost(2.5),
        name="last" if last else "next",
    )(meta, low_key, fast(q), fast(arrived[index]), *[fast(x) for x in state])
    return results[:2] if last else (results[:3], results[3])


def solution(mesh):
    placed = (
        P(("pack", "seq"), None),
        P(("pack", "seq"), None),
        P(("pack", "seq"), None),
        P("pack"),
        P("pack"),
    )
    return jax.shard_map(
        local, mesh=mesh, in_specs=placed, out_specs=P(("pack", "seq"), None), check_vma=False
    )
```

profile of v0, /device:TPU:259, one launch (start us, length us, event | category | flops | bytes accessed | tf_op | source)
XLA Modules:
  0.0 65.1 jit_solution(11755910264921754146)
XLA Ops:
  0.0 0.0 copy-start
  0.0 0.0 copy-start.1
  0.0 1.0 %near.1 = bf16[256,512]{1,0:T(8,128)(2,1)S(1)} custom-call(bf16[256,512]{1,0:T(8,128)(2,1)} %k.3, bf16[256,512]{1,0:T(8,128)(2,1)} %v.3), custom_call_target="tpu_custom_call" | custom-call | tf_op jit(solution)/shard_map/near/pallas_call | solution.py:289
  1.0 3.2 %collective-permute-start.3 = (bf16[256,512]{1,0:T(8,128)(2,1)S(1)}, bf16[256,512]{1,0:T(8,128)(2,1)S(1)}, u32[]{:S(2)}, u32[]{:S(2)}) collective-permute-start(bf16[256,512]{1,0:T(8,128)(2,1)S(1)} %near.1), channel_id=1, source_target_pairs={{0,8},{4,12},{8,16},{12,20},{16,24},{20,28},{24,32},{28,36},{32,40... | collective-permute-start | bytes 786440 | tf_op jit(solution)/shard_map/ppermute | solution.py:316
  4.2 1.5 %pack.1 = (bf16[256,512]{1,0:T(8,128)(2,1)S(1)}, bf16[256,1536]{1,0:T(8,128)(2,1)S(1)}, bf16[256,1024]{1,0:T(8,128)(2,1)S(1)}) custom-call(bf16[256,2048]{1,0:T(8,128)(2,1)} %q.1, bf16[256,512]{1,0:T(8,128)(2,1)} %k.3, bf16[256,512]{1,0:T(8,128)(2,1)} %v.3, bf16[256,512]{1,0:T(8,128)(2,1)S(1)} %near.1), custom_call_target="tpu_custom_call" | custom-call | tf_op jit(solution)/shard_map/pack/pallas_call | solution.py:298
  5.7 4.0 %collective-permute-start.1 = (bf16[256,512]{1,0:T(8,128)(2,1)S(1)}, bf16[256,512]{1,0:T(8,128)(2,1)S(1)}, u32[]{:S(2)}, u32[]{:S(2)}) collective-permute-start(bf16[256,512]{1,0:T(8,128)(2,1)S(1)} %get-tuple-element.47), channel_id=1, source_target_pairs={{0,12},{4,8},{8,20},{12,16},{16,28},{20,24},{24,36},{28,32},{32,44... | collective-permute-start | bytes 786440 | tf_op jit(solution)/shard_map/ppermute | solution.py:316
  9.8 1.9 %collective-permute-start = (bf16[256,1536]{1,0:T(8,128)(2,1)S(1)}, bf16[256,1536]{1,0:T(8,128)(2,1)S(1)}, u32[]{:S(2)}, u32[]{:S(2)}) collective-permute-start(bf16[256,1536]{1,0:T(8,128)(2,1)S(1)} %get-tuple-element.45), channel_id=1, source_target_pairs={{0,4},{4,0},{8,12},{12,8},{16,20},{20,16},{24,28},{28,24},{32,36},... | collective-permute-start | bytes 2359304 | tf_op jit(solution)/shard_map/ppermute | solution.py:317
  11.7 0.0 copy-done
  11.7 0.0 copy-done.1
  11.7 0.8 %plan.1 = (s32[32]{0:T(128)S(4)}, s32[512,128]{1,0:T(8,128)S(1)}) custom-call(s32[1,128]{1,0:T(1,128)S(1)} %bitcast.1, s32[256]{0:T(256)S(1)} %copy-done), custom_call_target="tpu_custom_call" | custom-call | flops 23000000512 | bytes 1048576 | tf_op jit(solution)/shard_map/plan/pallas_call | solution.py:319
  12.6 0.8 %collective-permute-done.3.kv = bf16[256,512]{1,0:T(8,128)(2,1)S(1)} collective-permute-done((bf16[256,512]{1,0:T(8,128)(2,1)S(1)}, bf16[256,512]{1,0:T(8,128)(2,1)S(1)}, u32[]{:S(2)}, u32[]{:S(2)}) %collective-permute-start.3) | collective-permute-done | bytes 262176 | tf_op jit(solution)/shard_map/ppermute | solution.py:316
  13.4 2.4 %collective-permute-start.5 = (bf16[256,512]{1,0:T(8,128)(2,1)S(1)}, bf16[256,512]{1,0:T(8,128)(2,1)S(1)}, u32[]{:S(2)}, u32[]{:S(2)}) collective-permute-start(bf16[256,512]{1,0:T(8,128)(2,1)S(1)} %collective-permute-done.3.kv), channel_id=1, source_target_pairs={{0,8},{4,12},{8,16},{12,20},{16,24},{20,28},{24,32},{28,36},{32,40... | collective-permute-start | bytes 786440 | tf_op jit(solution)/shard_map/ppermute | solution.py:346
  15.8 0.0 collective-permute-done.recv
  15.8 3.1 %first.1 = (bf16[512,1024]{1,0:T(8,128)(2,1)S(1)}, f32[512,1024]{1,0:T(8,128)S(1)}, f32[512,1024]{1,0:T(8,128)S(1)}, f32[512,1024]{1,0:T(8,128)S(1)}, f32[8,128]{1,0:T(8,128)S(1)}) custom-call(s32[32]{0:T(128)S(4)} %get-tuple-element.42.meta, s32[512,128]{1,0:T(8,128)S(1)} %get-tuple-element.43.low_key, bf16[256,1024]{1,0:T(8,128)(2,1)S(1)} %get-tuple-element.44.own, ...), custom_call_target="tpu_custom_call" | custom-call | flops 3449999872 | bytes 1048576 | tf_op jit(solution)/shard_map/first/pallas_call | solution.py:331
  18.9 1.3 %collective-permute-done.1.buffer_ref = bf16[256,512]{1,0:T(8,128)(2,1)S(1)} collective-permute-done((bf16[256,512]{1,0:T(8,128)(2,1)S(1)}, bf16[256,512]{1,0:T(8,128)(2,1)S(1)}, u32[]{:S(2)}, u32[]{:S(2)}) %collective-permute-start.1) | collective-permute-done | bytes 262176 | tf_op jit(solution)/shard_map/ppermute | solution.py:316
  20.2 3.2 %collective-permute-start.2 = (bf16[256,512]{1,0:T(8,128)(2,1)S(1)}, bf16[256,512]{1,0:T(8,128)(2,1)S(1)}, u32[]{:S(2)}, u32[]{:S(2)}) collective-permute-start(bf16[256,512]{1,0:T(8,128)(2,1)S(1)} %touch.5.kv), channel_id=1, source_target_pairs={{0,8},{4,12},{8,16},{12,20},{16,24},{20,28},{24,32},{28,36},{32,40... | collective-permute-start | bytes 786440 | tf_op jit(solution)/shard_map/ppermute | solution.py:346
  23.4 2.1 %next.7 = (f32[512,1024]{1,0:T(8,128)S(1)}, f32[512,1024]{1,0:T(8,128)S(1)}, f32[512,1024]{1,0:T(8,128)S(1)}, f32[8,128]{1,0:T(8,128)S(1)}) custom-call(s32[32]{0:T(128)S(4)} %get-tuple-element.42.meta, s32[512,128]{1,0:T(8,128)S(1)} %get-tuple-element.43.low_key, ...), custom_call_target="tpu_custom_call", output_to_operand_aliasing={{0}: (4, {}), {1}: (5, {}), {2}: (6, {})} | custom-call | flops 2875000064 | bytes 1048576 | tf_op jit(solution)/shard_map/next/pallas_call | solution.py:370
  25.5 0.0 collective-permute-done.5.buffer_ref
  25.5 1.9 %collective-permute-start.7 = (bf16[256,512]{1,0:T(8,128)(2,1)S(1)}, bf16[256,512]{1,0:T(8,128)(2,1)S(1)}, u32[]{:S(2)}, u32[]{:S(2)}) collective-permute-start(bf16[256,512]{1,0:T(8,128)(2,1)S(1)} %touch.7.kv), channel_id=1, source_target_pairs={{0,8},{4,12},{8,16},{12,20},{16,24},{20,28},{24,32},{28,36},{32,40... | collective-permute-start | bytes 786440 | tf_op jit(solution)/shard_map/ppermute | solution.py:346
  27.5 0.1 next.8
  27.5 0.1 next.9
  27.6 5.3 %collective-permute-done.2.buffer_ref = bf16[256,512]{1,0:T(8,128)(2,1)S(1)} collective-permute-done((bf16[256,512]{1,0:T(8,128)(2,1)S(1)}, bf16[256,512]{1,0:T(8,128)(2,1)S(1)}, u32[]{:S(2)}, u32[]{:S(2)}) %collective-permute-start.2) | collective-permute-done | bytes 262176 | tf_op jit(solution)/shard_map/ppermute | solution.py:346
  32.9 1.9 %collective-permute-start.4 = (bf16[256,512]{1,0:T(8,128)(2,1)S(1)}, bf16[256,512]{1,0:T(8,128)(2,1)S(1)}, u32[]{:S(2)}, u32[]{:S(2)}) collective-permute-start(bf16[256,512]{1,0:T(8,128)(2,1)S(1)} %touch.6.kv), channel_id=1, source_target_pairs={{0,8},{4,12},{8,16},{12,20},{16,24},{20,28},{24,32},{28,36},{32,40... | collective-permute-start | bytes 786440 | tf_op jit(solution)/shard_map/ppermute | solution.py:346
  34.8 2.5 %collective-permute-done.7.buffer_ref = bf16[256,512]{1,0:T(8,128)(2,1)S(1)} collective-permute-done((bf16[256,512]{1,0:T(8,128)(2,1)S(1)}, bf16[256,512]{1,0:T(8,128)(2,1)S(1)}, u32[]{:S(2)}, u32[]{:S(2)}) %collective-permute-start.7) | collective-permute-done | bytes 262176 | tf_op jit(solution)/shard_map/ppermute | solution.py:346
  37.2 2.1 %collective-permute-start.8 = (bf16[256,512]{1,0:T(8,128)(2,1)S(1)}, bf16[256,512]{1,0:T(8,128)(2,1)S(1)}, u32[]{:S(2)}, u32[]{:S(2)}) collective-permute-start(bf16[256,512]{1,0:T(8,128)(2,1)S(1)} %touch.9.kv), channel_id=1, source_target_pairs={{0,8},{4,12},{8,16},{12,20},{16,24},{20,28},{24,32},{28,36},{32,40... | collective-permute-start | bytes 786440 | tf_op jit(solution)/shard_map/ppermute | solution.py:346
  39.3 0.1 next.10
  39.4 0.1 next.11
  39.5 5.0 %collective-permute-done.4.buffer_ref = bf16[256,512]{1,0:T(8,128)(2,1)S(1)} collective-permute-done((bf16[256,512]{1,0:T(8,128)(2,1)S(1)}, bf16[256,512]{1,0:T(8,128)(2,1)S(1)}, u32[]{:S(2)}, u32[]{:S(2)}) %collective-permute-start.4) | collective-permute-done | bytes 262176 | tf_op jit(solution)/shard_map/ppermute | solution.py:346
  44.5 1.9 %collective-permute-start.6 = (bf16[256,512]{1,0:T(8,128)(2,1)S(1)}, bf16[256,512]{1,0:T(8,128)(2,1)S(1)}, u32[]{:S(2)}, u32[]{:S(2)}) collective-permute-start(bf16[256,512]{1,0:T(8,128)(2,1)S(1)} %touch.8.kv), channel_id=1, source_target_pairs={{0,8},{4,12},{8,16},{12,20},{16,24},{20,28},{24,32},{28,36},{32,40... | collective-permute-start | bytes 786440 | tf_op jit(solution)/shard_map/ppermute | solution.py:346
  46.4 0.1 next.12
  46.4 3.8 %collective-permute-done.8.kv = bf16[256,512]{1,0:T(8,128)(2,1)S(1)} collective-permute-done((bf16[256,512]{1,0:T(8,128)(2,1)S(1)}, bf16[256,512]{1,0:T(8,128)(2,1)S(1)}, u32[]{:S(2)}, u32[]{:S(2)}) %collective-permute-start.8) | collective-permute-done | bytes 262176 | tf_op jit(solution)/shard_map/ppermute | solution.py:346
  50.3 4.6 %collective-permute-done.6.kv = bf16[256,512]{1,0:T(8,128)(2,1)S(1)} collective-permute-done((bf16[256,512]{1,0:T(8,128)(2,1)S(1)}, bf16[256,512]{1,0:T(8,128)(2,1)S(1)}, u32[]{:S(2)}, u32[]{:S(2)}) %collective-permute-start.6) | collective-permute-done | bytes 262176 | tf_op jit(solution)/shard_map/ppermute | solution.py:346
  54.9 0.9 %last.1 = (bf16[256,1024]{1,0:T(8,128)(2,1)S(1)}, bf16[256,1024]{1,0:T(8,128)(2,1)S(1)}, f32[512,1024]{1,0:T(8,128)S(1)}, f32[512,1024]{1,0:T(8,128)S(1)}, f32[512,1024]{1,0:T(8,128)S(1)}) custom-call(s32[32]{0:T(128)S(4)} %get-tuple-element.42.meta, ...), custom_call_target="tpu_custom_call", output_to_operand_aliasing={{2}: (4, {}), {3}: (5, {}), {4}: (6, {})} | custom-call | flops 2875000064 | bytes 1048576 | tf_op jit(solution)/shard_map/last/pallas_call | solution.py:370
  55.8 6.6 %collective-permute-start.9 = (bf16[256,1024]{1,0:T(8,128)(2,1)S(1)}, bf16[256,1024]{1,0:T(8,128)(2,1)S(1)}, u32[]{:S(2)}, u32[]{:S(2)}) collective-permute-start(bf16[256,1024]{1,0:T(8,128)(2,1)S(1)} %get-tuple-element.78), channel_id=1, source_target_pairs={{0,4},{4,0},{8,12},{12,8},{16,20},{20,16},{24,28},{28,24},{32,36},... | collective-permute-start | bytes 1572872 | tf_op jit(solution)/shard_map/ppermute | solution.py:354
  62.4 1.5 %collective-permute-done.9.got = bf16[256,1024]{1,0:T(8,128)(2,1)S(1)} collective-permute-done((bf16[256,1024]{1,0:T(8,128)(2,1)S(1)}, bf16[256,1024]{1,0:T(8,128)(2,1)S(1)}, u32[]{:S(2)}, u32[]{:S(2)}) %collective-permute-start.9) | collective-permute-done | bytes 524320 | tf_op jit(solution)/shard_map/ppermute | solution.py:354
  63.9 1.0 %join.1 = bf16[256,2048]{1,0:T(8,128)(2,1)} custom-call(bf16[256,1024]{1,0:T(8,128)(2,1)S(1)} %get-tuple-element.77.keep, bf16[256,1024]{1,0:T(8,128)(2,1)S(1)} %collective-permute-done.9.got), custom_call_target="tpu_custom_call" | custom-call | tf_op jit(solution)/shard_map/join/pallas_call | solution.py:355
  (6 shorter events, 0.0 us)
Async XLA Ops:
  0.0 11.7 %copy-start = (s32[256]{0:T(256)S(1)}, s32[256]{0:T(256)}, u32[]{:S(2)}) copy-start(s32[256]{0:T(256)} %home.1) | copy-start | bytes 3076
  0.0 11.7 %copy-start.1 = (s32[128]{0:T(128)S(1)}, s32[128]{0:T(128)}, u32[]{:S(2)}) copy-start(s32[128]{0:T(128)} %param.8) | copy-start | bytes 1540
  1.0 12.4 %collective-permute-start.3 = (bf16[256,512]{1,0:T(8,128)(2,1)S(1)}, bf16[256,512]{1,0:T(8,128)(2,1)S(1)}, u32[]{:S(2)}, u32[]{:S(2)}) collective-permute-start(bf16[256,512]{1,0:T(8,128)(2,1)S(1)} %near.1), channel_id=1, source_target_pairs={{0,8},{4,12},{8,16},{12,20},{16,24},{20,28},{24,32},{28,36},{32,40... | collective-permute-start | bytes 786440 | tf_op jit(solution)/shard_map/ppermute | solution.py:316
  5.7 14.4 %collective-permute-start.1 = (bf16[256,512]{1,0:T(8,128)(2,1)S(1)}, bf16[256,512]{1,0:T(8,128)(2,1)S(1)}, u32[]{:S(2)}, u32[]{:S(2)}) collective-permute-start(bf16[256,512]{1,0:T(8,128)(2,1)S(1)} %get-tuple-element.47), channel_id=1, source_target_pairs={{0,12},{4,8},{8,20},{12,16},{16,28},{20,24},{24,36},{28,32},{32,44... | collective-permute-start | bytes 786440 | tf_op jit(solution)/shard_map/ppermute | solution.py:316
  9.8 6.0 %collective-permute-start = (bf16[256,1536]{1,0:T(8,128)(2,1)S(1)}, bf16[256,1536]{1,0:T(8,128)(2,1)S(1)}, u32[]{:S(2)}, u32[]{:S(2)}) collective-permute-start(bf16[256,1536]{1,0:T(8,128)(2,1)S(1)} %get-tuple-element.45), channel_id=1, source_target_pairs={{0,4},{4,0},{8,12},{12,8},{16,20},{20,16},{24,28},{28,24},{32,36},... | collective-permute-start | bytes 2359304 | tf_op jit(solution)/shard_map/ppermute | solution.py:317
  13.4 12.1 %collective-permute-start.5 = (bf16[256,512]{1,0:T(8,128)(2,1)S(1)}, bf16[256,512]{1,0:T(8,128)(2,1)S(1)}, u32[]{:S(2)}, u32[]{:S(2)}) collective-permute-start(bf16[256,512]{1,0:T(8,128)(2,1)S(1)} %collective-permute-done.3.kv), channel_id=1, source_target_pairs={{0,8},{4,12},{8,16},{12,20},{16,24},{20,28},{24,32},{28,36},{32,40... | collective-permute-start | bytes 786440 | tf_op jit(solution)/shard_map/ppermute | solution.py:346
  20.2 12.7 %collective-permute-start.2 = (bf16[256,512]{1,0:T(8,128)(2,1)S(1)}, bf16[256,512]{1,0:T(8,128)(2,1)S(1)}, u32[]{:S(2)}, u32[]{:S(2)}) collective-permute-start(bf16[256,512]{1,0:T(8,128)(2,1)S(1)} %touch.5.kv), channel_id=1, source_target_pairs={{0,8},{4,12},{8,16},{12,20},{16,24},{20,28},{24,32},{28,36},{32,40... | collective-permute-start | bytes 786440 | tf_op jit(solution)/shard_map/ppermute | solution.py:346
  25.5 11.7 %collective-permute-start.7 = (bf16[256,512]{1,0:T(8,128)(2,1)S(1)}, bf16[256,512]{1,0:T(8,128)(2,1)S(1)}, u32[]{:S(2)}, u32[]{:S(2)}) collective-permute-start(bf16[256,512]{1,0:T(8,128)(2,1)S(1)} %touch.7.kv), channel_id=1, source_target_pairs={{0,8},{4,12},{8,16},{12,20},{16,24},{20,28},{24,32},{28,36},{32,40... | collective-permute-start | bytes 786440 | tf_op jit(solution)/shard_map/ppermute | solution.py:346
  32.9 11.6 %collective-permute-start.4 = (bf16[256,512]{1,0:T(8,128)(2,1)S(1)}, bf16[256,512]{1,0:T(8,128)(2,1)S(1)}, u32[]{:S(2)}, u32[]{:S(2)}) collective-permute-start(bf16[256,512]{1,0:T(8,128)(2,1)S(1)} %touch.6.kv), channel_id=1, source_target_pairs={{0,8},{4,12},{8,16},{12,20},{16,24},{20,28},{24,32},{28,36},{32,40... | collective-permute-start | bytes 786440 | tf_op jit(solution)/shard_map/ppermute | solution.py:346
  37.2 13.0 %collective-permute-start.8 = (bf16[256,512]{1,0:T(8,128)(2,1)S(1)}, bf16[256,512]{1,0:T(8,128)(2,1)S(1)}, u32[]{:S(2)}, u32[]{:S(2)}) collective-permute-start(bf16[256,512]{1,0:T(8,128)(2,1)S(1)} %touch.9.kv), channel_id=1, source_target_pairs={{0,8},{4,12},{8,16},{12,20},{16,24},{20,28},{24,32},{28,36},{32,40... | collective-permute-start | bytes 786440 | tf_op jit(solution)/shard_map/ppermute | solution.py:346
  44.5 10.4 %collective-permute-start.6 = (bf16[256,512]{1,0:T(8,128)(2,1)S(1)}, bf16[256,512]{1,0:T(8,128)(2,1)S(1)}, u32[]{:S(2)}, u32[]{:S(2)}) collective-permute-start(bf16[256,512]{1,0:T(8,128)(2,1)S(1)} %touch.8.kv), channel_id=1, source_target_pairs={{0,8},{4,12},{8,16},{12,20},{16,24},{20,28},{24,32},{28,36},{32,40... | collective-permute-start | bytes 786440 | tf_op jit(solution)/shard_map/ppermute | solution.py:346
  55.8 8.1 %collective-permute-start.9 = (bf16[256,1024]{1,0:T(8,128)(2,1)S(1)}, bf16[256,1024]{1,0:T(8,128)(2,1)S(1)}, u32[]{:S(2)}, u32[]{:S(2)}) collective-permute-start(bf16[256,1024]{1,0:T(8,128)(2,1)S(1)} %get-tuple-element.78), channel_id=1, source_target_pairs={{0,4},{4,0},{8,12},{12,8},{16,20},{20,16},{24,28},{28,24},{32,36},... | collective-permute-start | bytes 1572872 | tf_op jit(solution)/shard_map/ppermute | solution.py:354
where the time goes:
time: 65.5 us; the launch traced here: 65.1 us
  starting transfers between devices  29.1 us (44%)
  waiting for transfers between devices  24.8 us (38%)
  Pallas kernels  10.7 us (16%)
    ppermute x6, waiting for transfers between devices, local(): arrived.append(shift(kv, perm=same))  21.2 us
    ppermute x6, starting transfers between devices, local(): arrived.append(shift(kv, perm=same))  13.4 us
    ppermute x2, starting transfers between devices, local(): arrived = [shift(near, perm=same), shift(cross, perm=other)]  7.25 us
    ppermute x1, starting transfers between devices, local(): got = shift(send, perm=pair)  6.56 us
    pallas_call x8, Pallas kernels, step(): pl.pallas_call(functools.partial(kernel, index // 2 + 1, index % 2), out_...  3.34 us
    pallas_call x1, Pallas kernels, local(): pl.pallas_call(first_kernel, out_shape=[pltpu.VMEM((2 * ROWS, HALF), bf16...  3.06 us
    ppermute x2, waiting for transfers between devices, local(): arrived = [shift(near, perm=same), shift(cross, perm=other)]  2.13 us
    ppermute x1, starting transfers between devices, local(): recv = fast(shift(swap, perm=pair))  1.92 us
  transfers between devices with their start and end apart: 10, of which 8 were waited for; matrix products, arithmetic and copies ran while one was open for 0% of the time, Pallas kernels for 12%

commit v1 on v0

--- a/solution.py
+++ b/solution.py
@@ -54,34 +54,11 @@
     )(fast(buffer), fast(token))
 
 
-def near_kernel(k, v, near, sems):
-    core = lax.rem(lax.axis_index("seq"), 2)
-    cols = pl.ds(pl.multiple_of(core * 256, 256), 256)
-    copies = [
-        pltpu.make_async_copy(source.at[:, cols], near.at[:, i * 256 : i * 256 + 256], sems.at[i])
-        for i, source in enumerate((k, v))
-    ]
-    for copy in copies:
-        copy.start()
-    for copy in copies:
-        copy.wait()
-
-
-def pack_kernel(q, k, v, near, cross, swap, own, sems):
-    core = lax.rem(lax.axis_index("seq"), 2)
-    other = 1 - core
-
-    def cols(index, width):
-        return pl.ds(pl.multiple_of(index * width, width), width)
-
-    moves = [
-        (k.at[:, cols(other, 256)], cross.at[:, 0:256]),
-        (v.at[:, cols(other, 256)], cross.at[:, 256:512]),
-        (q.at[:, cols(other, HALF)], swap.at[:, 0:HALF]),
-        (k.at[:, cols(other, 256)], swap.at[:, HALF : HALF + 256]),
-        (v.at[:, cols(other, 256)], swap.at[:, HALF + 256 : HALF + 512]),
-        (q.at[:, cols(core, HALF)], own),
-    ]
+def span(index, width):
+    return pl.ds(pl.multiple_of(index * width, width), width)
+
+
+def run_copies(moves, sems):
     copies = [
         pltpu.make_async_copy(source, target, sems.at[i])
         for i, (source, target) in enumerate(moves)
@@ -90,6 +67,27 @@
         copy.start()
     for copy in copies:
         copy.wait()
+
+
+def near_kernel(k, v, near, cross, sems):
+    core = lax.rem(lax.axis_index("seq"), 2)
+    moves = []
+    for target, half in ((near, core), (cross, 1 - core)):
+        for i, source in enumerate((k, v)):
+            moves.append((source.at[:, span(half, 256)], target.at[:, i * 256 : i * 256 + 256]))
+    run_copies(moves, sems)
+
+
+def pack_kernel(q, cross, lengths, home, swap, own, lengths_here, home_here, sems):
+    core = lax.rem(lax.axis_index("seq"), 2)
+    moves = [
+        (q.at[:, span(1 - core, HALF)], swap.at[:, 0:HALF]),
+        (q.at[:, span(core, HALF)], own),
+        (cross, swap.at[:, HALF : HALF + KVW]),
+        (lengths, lengths_here),
+        (home, home_here),
+    ]
+    run_copies(moves, sems)
 
 
 def plan_kernel(lengths, home, meta, low_key):
@@ -139,10 +137,10 @@
     )
 
 
-def fold(q, kv, kv_row, state, row, bias=None, first=False, span=ROWS):
+def fold(q, kv, kv_row, state, row, bias=None, first=False, width=ROWS):
     acc, top, low = state
     rows = row_span(row)
-    key_rows = pl.ds(kv_row, span)
+    key_rows = pl.ds(kv_row, width)
     for kvh in range(HEADS // GROUP):
         keys = kv[key_rows, kvh * HD : (kvh + 1) * HD]
         vals = kv[key_rows, 256 + kvh * HD : 256 + (kvh + 1) * HD]
@@ -164,10 +162,10 @@
             old = stacked(top, rows, kvh)
             new = jnp.maximum(old, peak)
             keep = jnp.exp2(old - new)
-        weights = jnp.exp2(scores - jnp.concatenate([new] * (span // HD), axis=1))
+        weights = jnp.exp2(scores - jnp.concatenate([new] * (width // HD), axis=1))
         mixed = jnp.dot(weights.astype(jnp.bfloat16), vals, preferred_element_type=jnp.float32)
         part = weights[:, :HD]
-        if span > HD:
+        if width > HD:
             part = part + weights[:, HD:]
         for g in range(GROUP):
             cols = pl.ds((kvh * GROUP + g) * HD, HD)
@@ -255,7 +253,7 @@
             for head in range(HEADS):
                 cols = pl.ds(head * HD, HD)
                 total = jnp.sum(low[rows, cols], axis=1, keepdims=True)
-                ref[slot, cols] = (acc[rows, cols] / total).astype(jnp.bfloat16)
+                ref[slot, cols] = (acc[rows, cols] * (1.0 / total)).astype(jnp.bfloat16)
 
         @pl.when(meta[MINE + block] == 1)
         def _(write=write):
@@ -272,48 +270,45 @@
 
 def join_kernel(keep, got, out, sems):
     core = lax.rem(lax.axis_index("seq"), 2)
-    copies = []
-    for i, (source, half) in enumerate(((keep, core), (got, 1 - core))):
-        cols = pl.ds(pl.multiple_of(half * HALF, HALF), HALF)
-        copies.append(pltpu.make_async_copy(source, out.at[:, cols], sems.at[i]))
-    for copy in copies:
-        copy.start()
-    for copy in copies:
-        copy.wait()
+    run_copies(
+        [(keep, out.at[:, span(core, HALF)]), (got, out.at[:, span(1 - core, HALF)])], sems
+    )
 
 
 def local(queries, keys, values, lengths, home):
     count = lax.axis_size("seq")
     bf16 = jnp.bfloat16
     hbm = pl.BlockSpec(memory_space=pltpu.HBM)
-    near = pl.pallas_call(
+    near, cross = pl.pallas_call(
         near_kernel,
-        out_shape=pltpu.VMEM((ROWS, KVW), bf16),
+        out_shape=[pltpu.VMEM((ROWS, KVW), bf16)] * 2,
         in_specs=[hbm] * 2,
-        out_specs=VSPEC,
-        scratch_shapes=[pltpu.SemaphoreType.DMA((2,))],
+        out_specs=[VSPEC] * 2,
+        scratch_shapes=[pltpu.SemaphoreType.DMA((4,))],
         compiler_params=params(60 * 1024 * 1024),
         name="near",
     )(keys, values)
-    cross, swap, own = pl.pallas_call(
+    lengths = lengths[None, :]
+    swap, own, lengths, home = pl.pallas_call(
         pack_kernel,
         out_shape=[
-            pltpu.VMEM((ROWS, KVW), bf16),
             pltpu.VMEM((ROWS, HALF + KVW), bf16),
             pltpu.VMEM((ROWS, HALF), bf16),
+            pltpu.VMEM(lengths.shape, jnp.int32),
+            pltpu.SMEM(home.shape, jnp.int32),
         ],
-        in_specs=[hbm] * 3 + [ASPEC],
-        out_specs=[VSPEC] * 3,
-        scratch_shapes=[pltpu.SemaphoreType.DMA((6,))],
+        in_specs=[hbm, VSPEC, hbm, hbm],
+        out_specs=[VSPEC] * 3 + [SSPEC],
+        scratch_shapes=[pltpu.SemaphoreType.DMA((5,))],
         compiler_params=params(60 * 1024 * 1024),
         name="pack",
-    )(queries, keys, values, fast(near))
+    )(queries, fast(cross), lengths, home)
 
     same = [(i, i + 2) for i in range(count - 2)]
     other = [(i, (i ^ 1) + 2) for i in range(count - 2)]
     pair = [(i, i ^ 1) for i in range(count)]
     shift = functools.partial(lax.ppermute, axis_name="seq")
-    arrived = [shift(near, perm=same), shift(cross, perm=other)]
+    arrived = [shift(cross, perm=other), shift(near, perm=same)]
     recv = fast(shift(swap, perm=pair))
 
     meta, low_key = pl.pallas_call(
@@ -324,7 +319,7 @@
         compiler_params=params(),
         cost_estimate=cost(PLAN),
         name="plan",
-    )(lengths[None, :], home)
+    )(fast(lengths), pltpu.with_memory_space_constraint(home, pltpu.SMEM))
     meta = pltpu.with_memory_space_constraint(meta, pltpu.SMEM)
     low_key, own = fast(low_key), fast(own)
 
@@ -368,13 +363,13 @@
     kernel = last_kernel if last else next_kernel
     extra = [pltpu.VMEM((ROWS, HALF), jnp.bfloat16)] * 2 if last else []
     results = pl.pallas_call(
-        functools.partial(kernel, index // 2 + 1, index % 2),
+        functools.partial(kernel, index // 2 + 1, 1 - index % 2),
         out_shape=extra + STATE + ([] if last else TOKEN),
         in_specs=[SSPEC] + [VSPEC] * 6,
         out_specs=[VSPEC] * (len(extra) + 3) + ([] if last else [ASPEC]),
         input_output_aliases={4 + i: len(extra) + i for i in range(3)},
         compiler_params=params(),
-        cost_estimate=cost(2.5),
+        cost_estimate=cost(1.0),
         name="last" if last else "next",
     )(meta, low_key, fast(q), fast(arrived[index]), *[fast(x) for x in state])
     return results[:2] if last else (results[:3], results[3])

time: 65.5 us -> 66.2 us (1.011)
  the two profiles are of different devices: /device:TPU:259 before, /device:TPU:263 now
where the time goes in v1:
time: 66.2 us; the launch traced here: 65.9 us
  starting transfers between devices  24.6 us (37%)
  Pallas kernels  23.5 us (35%)
  waiting for transfers between devices  17.4 us (26%)
    pallas_call x8, Pallas kernels, step(): pl.pallas_call(functools.partial(kernel, index // 2 + 1, 1 - index % 2),...  16.7 us
    ppermute x6, waiting for transfers between devices, local(): arrived.append(shift(kv, perm=same))  11.8 us
    ppermute x6, starting transfers between devices, local(): arrived.append(shift(kv, perm=same))  11.6 us
    ppermute x2, starting transfers between devices, local(): arrived = [shift(cross, perm=other), shift(near, perm=same)]  6.97 us
    ppermute x2, waiting for transfers between devices, local(): arrived = [shift(cross, perm=other), shift(near, perm=same)]  4.07 us
    ppermute x1, starting transfers between devices, local(): got = shift(send, perm=pair)  3.98 us
    pallas_call x1, Pallas kernels, local(): pl.pallas_call(first_kernel, out_shape=[pltpu.VMEM((2 * ROWS, HALF), bf16...  3.1 us
    ppermute x1, starting transfers between devices, local(): recv = fast(shift(swap, perm=pair))  2.02 us
  transfers between devices with their start and end apart: 10, of which 8 were waited for; matrix products, arithmetic and copies ran while one was open for 0% of the time, Pallas kernels for 28%

profile of v1, /device:TPU:263, one launch (start us, length us, event | category | flops | bytes accessed | tf_op | source)
XLA Modules:
  0.0 65.9 jit_solution(8603751736003189522)
XLA Ops:
  0.0 1.1 %near.1 = (bf16[256,512]{1,0:T(8,128)(2,1)S(1)}, bf16[256,512]{1,0:T(8,128)(2,1)S(1)}) custom-call(bf16[256,512]{1,0:T(8,128)(2,1)} %k.1, bf16[256,512]{1,0:T(8,128)(2,1)} %v.1), custom_call_target="tpu_custom_call" | custom-call | tf_op jit(solution)/shard_map/near/pallas_call | solution.py:282
  1.1 3.8 %collective-permute-start.3 = (bf16[256,512]{1,0:T(8,128)(2,1)S(1)}, bf16[256,512]{1,0:T(8,128)(2,1)S(1)}, u32[]{:S(2)}, u32[]{:S(2)}) collective-permute-start(bf16[256,512]{1,0:T(8,128)(2,1)S(1)} %get-tuple-element.45.cross), channel_id=1, source_target_pairs={{0,12},{4,8},{8,20},{12,16},{16,28},{20,24},{24,36},{28,32},{32,44... | collective-permute-start | bytes 786440 | tf_op jit(solution)/shard_map/ppermute | solution.py:311
  4.9 3.2 %collective-permute-start.1 = (bf16[256,512]{1,0:T(8,128)(2,1)S(1)}, bf16[256,512]{1,0:T(8,128)(2,1)S(1)}, u32[]{:S(2)}, u32[]{:S(2)}) collective-permute-start(bf16[256,512]{1,0:T(8,128)(2,1)S(1)} %get-tuple-element.51.near), channel_id=1, source_target_pairs={{0,8},{4,12},{8,16},{12,20},{16,24},{20,28},{24,32},{28,36},{32,40... | collective-permute-start | bytes 786440 | tf_op jit(solution)/shard_map/ppermute | solution.py:311
  8.1 1.3 %pack.1 = (bf16[256,1536]{1,0:T(8,128)(2,1)S(1)}, bf16[256,1024]{1,0:T(8,128)(2,1)S(1)}, s32[1,128]{1,0:T(1,128)S(1)}, s32[256]{0:T(256)S(4)}) custom-call(bf16[256,2048]{1,0:T(8,128)(2,1)} %q.1, bf16[256,512]{1,0:T(8,128)(2,1)S(1)} %get-tuple-element.45.cross, s32[1,128]{1,0:T(1,128)} %bitcast.1, s32[256]{0:T(256)} %home.1), custom_call_target="tpu_custom_call" | custom-call | tf_op jit(solution)/shard_map/pack/pallas_call | solution.py:292
  9.4 2.0 %collective-permute-start = (bf16[256,1536]{1,0:T(8,128)(2,1)S(1)}, bf16[256,1536]{1,0:T(8,128)(2,1)S(1)}, u32[]{:S(2)}, u32[]{:S(2)}) collective-permute-start(bf16[256,1536]{1,0:T(8,128)(2,1)S(1)} %get-tuple-element.52), channel_id=1, source_target_pairs={{0,4},{4,0},{8,12},{12,8},{16,20},{20,16},{24,28},{28,24},{32,36},... | collective-permute-start | bytes 2359304 | tf_op jit(solution)/shard_map/ppermute | solution.py:312
  11.4 0.3 plan.1
  11.7 3.5 %collective-permute-done.3.kv = bf16[256,512]{1,0:T(8,128)(2,1)S(1)} collective-permute-done((bf16[256,512]{1,0:T(8,128)(2,1)S(1)}, bf16[256,512]{1,0:T(8,128)(2,1)S(1)}, u32[]{:S(2)}, u32[]{:S(2)}) %collective-permute-start.3) | collective-permute-done | bytes 262176 | tf_op jit(solution)/shard_map/ppermute | solution.py:311
  15.2 1.9 %collective-permute-start.5 = (bf16[256,512]{1,0:T(8,128)(2,1)S(1)}, bf16[256,512]{1,0:T(8,128)(2,1)S(1)}, u32[]{:S(2)}, u32[]{:S(2)}) collective-permute-start(bf16[256,512]{1,0:T(8,128)(2,1)S(1)} %collective-permute-done.3.kv), channel_id=1, source_target_pairs={{0,8},{4,12},{8,16},{12,20},{16,24},{20,28},{24,32},{28,36},{32,40... | collective-permute-start | bytes 786440 | tf_op jit(solution)/shard_map/ppermute | solution.py:341
  17.1 0.0 collective-permute-done.recv
  17.1 3.1 %first.1 = (bf16[512,1024]{1,0:T(8,128)(2,1)S(1)}, f32[512,1024]{1,0:T(8,128)S(1)}, f32[512,1024]{1,0:T(8,128)S(1)}, f32[512,1024]{1,0:T(8,128)S(1)}, f32[8,128]{1,0:T(8,128)S(1)}) custom-call(s32[32]{0:T(128)S(4)} %get-tuple-element.48.meta, s32[512,128]{1,0:T(8,128)S(1)} %get-tuple-element.49.low_key, bf16[256,1024]{1,0:T(8,128)(2,1)S(1)} %get-tuple-element.50.own, ...), custom_call_target="tpu_custom_call" | custom-call | flops 3449999872 | bytes 1048576 | tf_op jit(solution)/shard_map/first/pallas_call | solution.py:326
  20.3 0.6 collective-permute-done.1.buffer_ref
  20.8 1.9 %collective-permute-start.2 = (bf16[256,512]{1,0:T(8,128)(2,1)S(1)}, bf16[256,512]{1,0:T(8,128)(2,1)S(1)}, u32[]{:S(2)}, u32[]{:S(2)}) collective-permute-start(bf16[256,512]{1,0:T(8,128)(2,1)S(1)} %touch.5.kv), channel_id=1, source_target_pairs={{0,8},{4,12},{8,16},{12,20},{16,24},{20,28},{24,32},{28,36},{32,40... | collective-permute-start | bytes 786440 | tf_op jit(solution)/shard_map/ppermute | solution.py:341
  22.8 2.1 %next.7 = (f32[512,1024]{1,0:T(8,128)S(1)}, f32[512,1024]{1,0:T(8,128)S(1)}, f32[512,1024]{1,0:T(8,128)S(1)}, f32[8,128]{1,0:T(8,128)S(1)}) custom-call(s32[32]{0:T(128)S(4)} %get-tuple-element.48.meta, s32[512,128]{1,0:T(8,128)S(1)} %get-tuple-element.49.low_key, ...), custom_call_target="tpu_custom_call", output_to_operand_aliasing={{0}: (4, {}), {1}: (5, {}), {2}: (6, {})} | custom-call | flops 1150000000 | bytes 1048576 | tf_op jit(solution)/shard_map/next/pallas_call | solution.py:365
  24.9 3.0 %collective-permute-done.5.buffer_ref = bf16[256,512]{1,0:T(8,128)(2,1)S(1)} collective-permute-done((bf16[256,512]{1,0:T(8,128)(2,1)S(1)}, bf16[256,512]{1,0:T(8,128)(2,1)S(1)}, u32[]{:S(2)}, u32[]{:S(2)}) %collective-permute-start.5) | collective-permute-done | bytes 262176 | tf_op jit(solution)/shard_map/ppermute | solution.py:341
  27.9 1.9 %collective-permute-start.7 = (bf16[256,512]{1,0:T(8,128)(2,1)S(1)}, bf16[256,512]{1,0:T(8,128)(2,1)S(1)}, u32[]{:S(2)}, u32[]{:S(2)}) collective-permute-start(bf16[256,512]{1,0:T(8,128)(2,1)S(1)} %touch.7.kv), channel_id=1, source_target_pairs={{0,8},{4,12},{8,16},{12,20},{16,24},{20,28},{24,32},{28,36},{32,40... | collective-permute-start | bytes 786440 | tf_op jit(solution)/shard_map/ppermute | solution.py:341
  29.8 2.1 %next.8 = (f32[512,1024]{1,0:T(8,128)S(1)}, f32[512,1024]{1,0:T(8,128)S(1)}, f32[512,1024]{1,0:T(8,128)S(1)}, f32[8,128]{1,0:T(8,128)S(1)}) custom-call(s32[32]{0:T(128)S(4)} %get-tuple-element.48.meta, s32[512,128]{1,0:T(8,128)S(1)} %get-tuple-element.49.low_key, ...), custom_call_target="tpu_custom_call", output_to_operand_aliasing={{0}: (4, {}), {1}: (5, {}), {2}: (6, {})} | custom-call | flops 1150000000 | bytes 1048576 | tf_op jit(solution)/shard_map/next/pallas_call | solution.py:365
  31.9 1.6 %collective-permute-done.2.buffer_ref = bf16[256,512]{1,0:T(8,128)(2,1)S(1)} collective-permute-done((bf16[256,512]{1,0:T(8,128)(2,1)S(1)}, bf16[256,512]{1,0:T(8,128)(2,1)S(1)}, u32[]{:S(2)}, u32[]{:S(2)}) %collective-permute-start.2) | collective-permute-done | bytes 262176 | tf_op jit(solution)/shard_map/ppermute | solution.py:341
  33.5 1.9 %collective-permute-start.4 = (bf16[256,512]{1,0:T(8,128)(2,1)S(1)}, bf16[256,512]{1,0:T(8,128)(2,1)S(1)}, u32[]{:S(2)}, u32[]{:S(2)}) collective-permute-start(bf16[256,512]{1,0:T(8,128)(2,1)S(1)} %touch.6.kv), channel_id=1, source_target_pairs={{0,8},{4,12},{8,16},{12,20},{16,24},{20,28},{24,32},{28,36},{32,40... | collective-permute-start | bytes 786440 | tf_op jit(solution)/shard_map/ppermute | solution.py:341
  35.4 2.1 %next.9 = (f32[512,1024]{1,0:T(8,128)S(1)}, f32[512,1024]{1,0:T(8,128)S(1)}, f32[512,1024]{1,0:T(8,128)S(1)}, f32[8,128]{1,0:T(8,128)S(1)}) custom-call(s32[32]{0:T(128)S(4)} %get-tuple-element.48.meta, s32[512,128]{1,0:T(8,128)S(1)} %get-tuple-element.49.low_key, ...), custom_call_target="tpu_custom_call", output_to_operand_aliasing={{0}: (4, {}), {1}: (5, {}), {2}: (6, {})} | custom-call | flops 1150000000 | bytes 1048576 | tf_op jit(solution)/shard_map/next/pallas_call | solution.py:365
  37.5 2.1 %collective-permute-done.7.buffer_ref = bf16[256,512]{1,0:T(8,128)(2,1)S(1)} collective-permute-done((bf16[256,512]{1,0:T(8,128)(2,1)S(1)}, bf16[256,512]{1,0:T(8,128)(2,1)S(1)}, u32[]{:S(2)}, u32[]{:S(2)}) %collective-permute-start.7) | collective-permute-done | bytes 262176 | tf_op jit(solution)/shard_map/ppermute | solution.py:341
  39.7 1.9 %collective-permute-start.8 = (bf16[256,512]{1,0:T(8,128)(2,1)S(1)}, bf16[256,512]{1,0:T(8,128)(2,1)S(1)}, u32[]{:S(2)}, u32[]{:S(2)}) collective-permute-start(bf16[256,512]{1,0:T(8,128)(2,1)S(1)} %touch.9.kv), channel_id=1, source_target_pairs={{0,8},{4,12},{8,16},{12,20},{16,24},{20,28},{24,32},{28,36},{32,40... | collective-permute-start | bytes 786440 | tf_op jit(solution)/shard_map/ppermute | solution.py:341
  41.6 2.1 %next.10 = (f32[512,1024]{1,0:T(8,128)S(1)}, f32[512,1024]{1,0:T(8,128)S(1)}, f32[512,1024]{1,0:T(8,128)S(1)}, f32[8,128]{1,0:T(8,128)S(1)}) custom-call(s32[32]{0:T(128)S(4)} %get-tuple-element.48.meta, s32[512,128]{1,0:T(8,128)S(1)} %get-tuple-element.49.low_key, ...), custom_call_target="tpu_custom_call", output_to_operand_aliasing={{0}: (4, {}), {1}: (5, {}), {2}: (6, {})} | custom-call | flops 1150000000 | bytes 1048576 | tf_op jit(solution)/shard_map/next/pallas_call | solution.py:365
  43.7 1.6 %collective-permute-done.4.buffer_ref = bf16[256,512]{1,0:T(8,128)(2,1)S(1)} collective-permute-done((bf16[256,512]{1,0:T(8,128)(2,1)S(1)}, bf16[256,512]{1,0:T(8,128)(2,1)S(1)}, u32[]{:S(2)}, u32[]{:S(2)}) %collective-permute-start.4) | collective-permute-done | bytes 262176 | tf_op jit(solution)/shard_map/ppermute | solution.py:341
  45.3 2.1 %collective-permute-start.6 = (bf16[256,512]{1,0:T(8,128)(2,1)S(1)}, bf16[256,512]{1,0:T(8,128)(2,1)S(1)}, u32[]{:S(2)}, u32[]{:S(2)}) collective-permute-start(bf16[256,512]{1,0:T(8,128)(2,1)S(1)} %touch.8.kv), channel_id=1, source_target_pairs={{0,8},{4,12},{8,16},{12,20},{16,24},{20,28},{24,32},{28,36},{32,40... | collective-permute-start | bytes 786440 | tf_op jit(solution)/shard_map/ppermute | solution.py:341
  47.4 2.1 %next.11 = (f32[512,1024]{1,0:T(8,128)S(1)}, f32[512,1024]{1,0:T(8,128)S(1)}, f32[512,1024]{1,0:T(8,128)S(1)}, f32[8,128]{1,0:T(8,128)}) custom-call(s32[32]{0:T(128)S(4)} %get-tuple-element.48.meta, s32[512,128]{1,0:T(8,128)S(1)} %get-tuple-element.49.low_key, ...), custom_call_target="tpu_custom_call", output_to_operand_aliasing={{0}: (4, {}), {1}: (5, {}), {2}: (6, {})} | custom-call | flops 1150000000 | bytes 1048576 | tf_op jit(solution)/shard_map/next/pallas_call | solution.py:365
  49.5 2.1 %next.12 = (f32[512,1024]{1,0:T(8,128)S(1)}, f32[512,1024]{1,0:T(8,128)S(1)}, f32[512,1024]{1,0:T(8,128)S(1)}, f32[8,128]{1,0:T(8,128)}) custom-call(s32[32]{0:T(128)S(4)} %get-tuple-element.48.meta, s32[512,128]{1,0:T(8,128)S(1)} %get-tuple-element.49.low_key, ...), custom_call_target="tpu_custom_call", output_to_operand_aliasing={{0}: (4, {}), {1}: (5, {}), {2}: (6, {})} | custom-call | flops 1150000000 | bytes 1048576 | tf_op jit(solution)/shard_map/next/pallas_call | solution.py:365
  51.6 0.0 collective-permute-done.8.kv
  51.6 1.1 %next.13 = (f32[512,1024]{1,0:T(8,128)S(1)}, f32[512,1024]{1,0:T(8,128)S(1)}, f32[512,1024]{1,0:T(8,128)S(1)}, f32[8,128]{1,0:T(8,128)}) custom-call(s32[32]{0:T(128)S(4)} %get-tuple-element.48.meta, s32[512,128]{1,0:T(8,128)S(1)} %get-tuple-element.49.low_key, ...), custom_call_target="tpu_custom_call", output_to_operand_aliasing={{0}: (4, {}), {1}: (5, {}), {2}: (6, {})} | custom-call | flops 1150000000 | bytes 1048576 | tf_op jit(solution)/shard_map/next/pallas_call | solution.py:365
  52.7 3.4 %collective-permute-done.6.kv = bf16[256,512]{1,0:T(8,128)(2,1)S(1)} collective-permute-done((bf16[256,512]{1,0:T(8,128)(2,1)S(1)}, bf16[256,512]{1,0:T(8,128)(2,1)S(1)}, u32[]{:S(2)}, u32[]{:S(2)}) %collective-permute-start.6) | collective-permute-done | bytes 262176 | tf_op jit(solution)/shard_map/ppermute | solution.py:341
  56.2 3.0 %last.1 = (bf16[256,1024]{1,0:T(8,128)(2,1)S(1)}, bf16[256,1024]{1,0:T(8,128)(2,1)S(1)}, f32[512,1024]{1,0:T(8,128)S(1)}, f32[512,1024]{1,0:T(8,128)S(1)}, f32[512,1024]{1,0:T(8,128)S(1)}) custom-call(s32[32]{0:T(128)S(4)} %get-tuple-element.48.meta, ...), custom_call_target="tpu_custom_call", output_to_operand_aliasing={{2}: (4, {}), {3}: (5, {}), {4}: (6, {})} | custom-call | flops 1150000000 | bytes 1048576 | tf_op jit(solution)/shard_map/last/pallas_call | solution.py:365
  59.2 4.0 %collective-permute-start.9 = (bf16[256,1024]{1,0:T(8,128)(2,1)S(1)}, bf16[256,1024]{1,0:T(8,128)(2,1)S(1)}, u32[]{:S(2)}, u32[]{:S(2)}) collective-permute-start(bf16[256,1024]{1,0:T(8,128)(2,1)S(1)} %get-tuple-element.84), channel_id=1, source_target_pairs={{0,4},{4,0},{8,12},{12,8},{16,20},{20,16},{24,28},{28,24},{32,36},... | collective-permute-start | bytes 1572872 | tf_op jit(solution)/shard_map/ppermute | solution.py:349
  63.2 1.5 %collective-permute-done.9.got = bf16[256,1024]{1,0:T(8,128)(2,1)S(1)} collective-permute-done((bf16[256,1024]{1,0:T(8,128)(2,1)S(1)}, bf16[256,1024]{1,0:T(8,128)(2,1)S(1)}, u32[]{:S(2)}, u32[]{:S(2)}) %collective-permute-start.9) | collective-permute-done | bytes 524320 | tf_op jit(solution)/shard_map/ppermute | solution.py:349
  64.7 1.0 %join.1 = bf16[256,2048]{1,0:T(8,128)(2,1)} custom-call(bf16[256,1024]{1,0:T(8,128)(2,1)S(1)} %get-tuple-element.83.keep, bf16[256,1024]{1,0:T(8,128)(2,1)S(1)} %collective-permute-done.9.got), custom_call_target="tpu_custom_call" | custom-call | tf_op jit(solution)/shard_map/join/pallas_call | solution.py:350
  (5 shorter events, 0.0 us)
Async XLA Ops:
  1.1 14.1 %collective-permute-start.3 = (bf16[256,512]{1,0:T(8,128)(2,1)S(1)}, bf16[256,512]{1,0:T(8,128)(2,1)S(1)}, u32[]{:S(2)}, u32[]{:S(2)}) collective-permute-start(bf16[256,512]{1,0:T(8,128)(2,1)S(1)} %get-tuple-element.45.cross), channel_id=1, source_target_pairs={{0,12},{4,8},{8,20},{12,16},{16,28},{20,24},{24,36},{28,32},{32,44... | collective-permute-start | bytes 786440 | tf_op jit(solution)/shard_map/ppermute | solution.py:311
  4.9 15.9 %collective-permute-start.1 = (bf16[256,512]{1,0:T(8,128)(2,1)S(1)}, bf16[256,512]{1,0:T(8,128)(2,1)S(1)}, u32[]{:S(2)}, u32[]{:S(2)}) collective-permute-start(bf16[256,512]{1,0:T(8,128)(2,1)S(1)} %get-tuple-element.51.near), channel_id=1, source_target_pairs={{0,8},{4,12},{8,16},{12,20},{16,24},{20,28},{24,32},{28,36},{32,40... | collective-permute-start | bytes 786440 | tf_op jit(solution)/shard_map/ppermute | solution.py:311
  9.4 7.7 %collective-permute-start = (bf16[256,1536]{1,0:T(8,128)(2,1)S(1)}, bf16[256,1536]{1,0:T(8,128)(2,1)S(1)}, u32[]{:S(2)}, u32[]{:S(2)}) collective-permute-start(bf16[256,1536]{1,0:T(8,128)(2,1)S(1)} %get-tuple-element.52), channel_id=1, source_target_pairs={{0,4},{4,0},{8,12},{12,8},{16,20},{20,16},{24,28},{28,24},{32,36},... | collective-permute-start | bytes 2359304 | tf_op jit(solution)/shard_map/ppermute | solution.py:312
  15.2 12.7 %collective-permute-start.5 = (bf16[256,512]{1,0:T(8,128)(2,1)S(1)}, bf16[256,512]{1,0:T(8,128)(2,1)S(1)}, u32[]{:S(2)}, u32[]{:S(2)}) collective-permute-start(bf16[256,512]{1,0:T(8,128)(2,1)S(1)} %collective-permute-done.3.kv), channel_id=1, source_target_pairs={{0,8},{4,12},{8,16},{12,20},{16,24},{20,28},{24,32},{28,36},{32,40... | collective-permute-start | bytes 786440 | tf_op jit(solution)/shard_map/ppermute | solution.py:341
  20.8 12.7 %collective-permute-start.2 = (bf16[256,512]{1,0:T(8,128)(2,1)S(1)}, bf16[256,512]{1,0:T(8,128)(2,1)S(1)}, u32[]{:S(2)}, u32[]{:S(2)}) collective-permute-start(bf16[256,512]{1,0:T(8,128)(2,1)S(1)} %touch.5.kv), channel_id=1, source_target_pairs={{0,8},{4,12},{8,16},{12,20},{16,24},{20,28},{24,32},{28,36},{32,40... | collective-permute-start | bytes 786440 | tf_op jit(solution)/shard_map/ppermute | solution.py:341
  27.9 11.8 %collective-permute-start.7 = (bf16[256,512]{1,0:T(8,128)(2,1)S(1)}, bf16[256,512]{1,0:T(8,128)(2,1)S(1)}, u32[]{:S(2)}, u32[]{:S(2)}) collective-permute-start(bf16[256,512]{1,0:T(8,128)(2,1)S(1)} %touch.7.kv), channel_id=1, source_target_pairs={{0,8},{4,12},{8,16},{12,20},{16,24},{20,28},{24,32},{28,36},{32,40... | collective-permute-start | bytes 786440 | tf_op jit(solution)/shard_map/ppermute | solution.py:341
  33.5 11.8 %collective-permute-start.4 = (bf16[256,512]{1,0:T(8,128)(2,1)S(1)}, bf16[256,512]{1,0:T(8,128)(2,1)S(1)}, u32[]{:S(2)}, u32[]{:S(2)}) collective-permute-start(bf16[256,512]{1,0:T(8,128)(2,1)S(1)} %touch.6.kv), channel_id=1, source_target_pairs={{0,8},{4,12},{8,16},{12,20},{16,24},{20,28},{24,32},{28,36},{32,40... | collective-permute-start | bytes 786440 | tf_op jit(solution)/shard_map/ppermute | solution.py:341
  39.7 11.9 %collective-permute-start.8 = (bf16[256,512]{1,0:T(8,128)(2,1)S(1)}, bf16[256,512]{1,0:T(8,128)(2,1)S(1)}, u32[]{:S(2)}, u32[]{:S(2)}) collective-permute-start(bf16[256,512]{1,0:T(8,128)(2,1)S(1)} %touch.9.kv), channel_id=1, source_target_pairs={{0,8},{4,12},{8,16},{12,20},{16,24},{20,28},{24,32},{28,36},{32,40... | collective-permute-start | bytes 786440 | tf_op jit(solution)/shard_map/ppermute | solution.py:341
  45.3 10.9 %collective-permute-start.6 = (bf16[256,512]{1,0:T(8,128)(2,1)S(1)}, bf16[256,512]{1,0:T(8,128)(2,1)S(1)}, u32[]{:S(2)}, u32[]{:S(2)}) collective-permute-start(bf16[256,512]{1,0:T(8,128)(2,1)S(1)} %touch.8.kv), channel_id=1, source_target_pairs={{0,8},{4,12},{8,16},{12,20},{16,24},{20,28},{24,32},{28,36},{32,40... | collective-permute-start | bytes 786440 | tf_op jit(solution)/shard_map/ppermute | solution.py:341
  59.2 5.5 %collective-permute-start.9 = (bf16[256,1024]{1,0:T(8,128)(2,1)S(1)}, bf16[256,1024]{1,0:T(8,128)(2,1)S(1)}, u32[]{:S(2)}, u32[]{:S(2)}) collective-permute-start(bf16[256,1024]{1,0:T(8,128)(2,1)S(1)} %get-tuple-element.84), channel_id=1, source_target_pairs={{0,4},{4,0},{8,12},{12,8},{16,20},{20,16},{24,28},{28,24},{32,36},... | collective-permute-start | bytes 1572872 | tf_op jit(solution)/shard_map/ppermute | solution.py:349

commit v2 on v1

--- a/solution.py
+++ b/solution.py
@@ -242,37 +242,36 @@
     lax.fori_loop(0, 2, body, 0)
 
 
-def last_kernel(back, side, meta, low_key, q, kv, a, t, d, keep, send, acc, top, low):
-    next_kernel(back, side, meta, low_key, q, kv, a, t, d, acc, top, low)
-
+def write_blocks(meta, acc, low, target, mine):
     def body(block, carry):
         rows = row_span(block * BLOCK)
-        slot = pl.ds(pl.multiple_of(meta[SLOT + block] * BLOCK, BLOCK), BLOCK)
-
-        def write(ref, rows=rows, slot=slot):
+        slot = row_span(meta[SLOT + block] * BLOCK)
+
+        @pl.when(meta[MINE + block] == mine)
+        def _():
             for head in range(HEADS):
                 cols = pl.ds(head * HD, HD)
                 total = jnp.sum(low[rows, cols], axis=1, keepdims=True)
-                ref[slot, cols] = (acc[rows, cols] * (1.0 / total)).astype(jnp.bfloat16)
-
-        @pl.when(meta[MINE + block] == 1)
-        def _(write=write):
-            write(keep)
-
-        @pl.when(meta[MINE + block] == 0)
-        def _(write=write):
-            write(send)
+                target[slot, cols] = (acc[rows, cols] * (1.0 / total)).astype(jnp.bfloat16)
 
         return carry
 
     lax.fori_loop(0, 4, body, 0)
 
 
-def join_kernel(keep, got, out, sems):
+def last_kernel(back, side, meta, low_key, q, kv, a, t, d, send, acc, top, low):
+    next_kernel(back, side, meta, low_key, q, kv, a, t, d, acc, top, low)
+    write_blocks(meta, acc, low, send, 0)
+
+
+def keep_kernel(meta, acc, low, out, kept, sems):
+    write_blocks(meta, acc, low, kept, 1)
+    run_copies([(kept, out.at[:, span(meta[0], HALF)])], sems)
+
+
+def join_kernel(got, partial, out, sems):
     core = lax.rem(lax.axis_index("seq"), 2)
-    run_copies(
-        [(keep, out.at[:, span(core, HALF)]), (got, out.at[:, span(1 - core, HALF)])], sems
-    )
+    run_copies([(got, out.at[:, span(1 - core, HALF)])], sems)
 
 
 def local(queries, keys, values, lengths, home):
@@ -345,23 +344,34 @@
         tokens.append(token)
     for index in (5, 6):
         state, token = step(index, arrived, meta, low_key, q, state)
-    keep, send = step(7, arrived, meta, low_key, q, state)
+    send, acc, low = step(7, arrived, meta, low_key, q, state)
     got = shift(send, perm=pair)
+    partial = pl.pallas_call(
+        keep_kernel,
+        out_shape=pltpu.HBM((ROWS, 2 * HALF), bf16),
+        in_specs=[SSPEC, VSPEC, VSPEC],
+        out_specs=hbm,
+        scratch_shapes=[pltpu.VMEM((ROWS, HALF), bf16), pltpu.SemaphoreType.DMA((1,))],
+        compiler_params=params(),
+        cost_estimate=cost(0.5),
+        name="keep",
+    )(meta, fast(acc), fast(low))
     return pl.pallas_call(
         join_kernel,
         out_shape=jax.ShapeDtypeStruct((ROWS, 2 * HALF), bf16),
-        in_specs=[VSPEC] * 2,
-        out_specs=pl.BlockSpec(memory_space=pltpu.HBM),
-        scratch_shapes=[pltpu.SemaphoreType.DMA((2,))],
+        in_specs=[VSPEC, hbm],
+        out_specs=hbm,
+        input_output_aliases={1: 0},
+        scratch_shapes=[pltpu.SemaphoreType.DMA((1,))],
         compiler_params=params(),
         name="join",
-    )(fast(keep), fast(got))
+    )(fast(got), partial)
 
 
 def step(index, arrived, meta, low_key, q, state):
     last = index == 7
     kernel = last_kernel if last else next_kernel
-    extra = [pltpu.VMEM((ROWS, HALF), jnp.bfloat16)] * 2 if last else []
+    extra = [pltpu.VMEM((ROWS, HALF), jnp.bfloat16)] if last else []
     results = pl.pallas_call(
         functools.partial(kernel, index // 2 + 1, 1 - index % 2),
         out_shape=extra + STATE + ([] if last else TOKEN),
@@ -372,7 +382,7 @@
         cost_estimate=cost(1.0),
         name="last" if last else "next",
     )(meta, low_key, fast(q), fast(arrived[index]), *[fast(x) for x in state])
-    return results[:2] if last else (results[:3], results[3])
+    return (results[0], results[1], results[3]) if last else (results[:3], results[3])
 
 
 def solution(mesh):

time: 66.2 us -> 65.1 us (0.983)
  the two profiles are of different devices: /device:TPU:263 before, /device:TPU:257 now
where the time goes in v2:
time: 65.1 us; the launch traced here: 64.8 us
  starting transfers between devices  24.9 us (38%)
  waiting for transfers between devices  24.8 us (38%)
  Pallas kernels  14.8 us (23%)
    ppermute x6, waiting for transfers between devices, local(): arrived.append(shift(kv, perm=same))  20.5 us
    ppermute x6, starting transfers between devices, local(): arrived.append(shift(kv, perm=same))  11.6 us
    ppermute x2, starting transfers between devices, local(): arrived = [shift(cross, perm=other), shift(near, perm=same)]  6.97 us
    pallas_call x8, Pallas kernels, step(): pl.pallas_call(functools.partial(kernel, index // 2 + 1, 1 - index % 2),...  6.89 us
    ppermute x1, starting transfers between devices, local(): got = shift(send, perm=pair)  4.35 us
    ppermute x2, waiting for transfers between devices, local(): arrived = [shift(cross, perm=other), shift(near, perm=same)]  4.06 us
    pallas_call x1, Pallas kernels, local(): pl.pallas_call(first_kernel, out_shape=[pltpu.VMEM((2 * ROWS, HALF), bf16...  3.08 us
    ppermute x1, starting transfers between devices, local(): recv = fast(shift(swap, perm=pair))  1.92 us
  transfers between devices with their start and end apart: 10, of which 9 were waited for; matrix products, arithmetic and copies ran while one was open for 0% of the time, Pallas kernels for 19%

profile of v2, /device:TPU:257, one launch (start us, length us, event | category | flops | bytes accessed | tf_op | source)
XLA Modules:
  0.0 64.8 jit_solution(1326301968854833973)
XLA Ops:
  0.0 1.1 %near.1 = (bf16[256,512]{1,0:T(8,128)(2,1)S(1)}, bf16[256,512]{1,0:T(8,128)(2,1)S(1)}) custom-call(bf16[256,512]{1,0:T(8,128)(2,1)} %k.1, bf16[256,512]{1,0:T(8,128)(2,1)} %v.1), custom_call_target="tpu_custom_call" | custom-call | tf_op jit(solution)/shard_map/near/pallas_call | solution.py:281
  1.1 3.8 %collective-permute-start.3 = (bf16[256,512]{1,0:T(8,128)(2,1)S(1)}, bf16[256,512]{1,0:T(8,128)(2,1)S(1)}, u32[]{:S(2)}, u32[]{:S(2)}) collective-permute-start(bf16[256,512]{1,0:T(8,128)(2,1)S(1)} %get-tuple-element.46.cross), channel_id=1, source_target_pairs={{0,12},{4,8},{8,20},{12,16},{16,28},{20,24},{24,36},{28,32},{32,44... | collective-permute-start | bytes 786440 | tf_op jit(solution)/shard_map/ppermute | solution.py:310
  4.9 1.3 %pack.1 = (bf16[256,1536]{1,0:T(8,128)(2,1)S(1)}, bf16[256,1024]{1,0:T(8,128)(2,1)S(1)}, s32[1,128]{1,0:T(1,128)S(1)}, s32[256]{0:T(256)S(4)}) custom-call(bf16[256,2048]{1,0:T(8,128)(2,1)} %q.1, bf16[256,512]{1,0:T(8,128)(2,1)S(1)} %get-tuple-element.46.cross, s32[1,128]{1,0:T(1,128)} %bitcast.1, s32[256]{0:T(256)} %home.1), custom_call_target="tpu_custom_call" | custom-call | tf_op jit(solution)/shard_map/pack/pallas_call | solution.py:291
  6.2 1.9 %collective-permute-start = (bf16[256,1536]{1,0:T(8,128)(2,1)S(1)}, bf16[256,1536]{1,0:T(8,128)(2,1)S(1)}, u32[]{:S(2)}, u32[]{:S(2)}) collective-permute-start(bf16[256,1536]{1,0:T(8,128)(2,1)S(1)} %get-tuple-element.53), channel_id=1, source_target_pairs={{0,4},{4,0},{8,12},{12,8},{16,20},{20,16},{24,28},{28,24},{32,36},... | collective-permute-start | bytes 2359304 | tf_op jit(solution)/shard_map/ppermute | solution.py:311
  8.1 3.2 %collective-permute-start.1 = (bf16[256,512]{1,0:T(8,128)(2,1)S(1)}, bf16[256,512]{1,0:T(8,128)(2,1)S(1)}, u32[]{:S(2)}, u32[]{:S(2)}) collective-permute-start(bf16[256,512]{1,0:T(8,128)(2,1)S(1)} %get-tuple-element.52.near), channel_id=1, source_target_pairs={{0,8},{4,12},{8,16},{12,20},{16,24},{20,28},{24,32},{28,36},{32,40... | collective-permute-start | bytes 786440 | tf_op jit(solution)/shard_map/ppermute | solution.py:310
  11.3 0.3 plan.1
  11.6 3.6 %collective-permute-done.3.kv = bf16[256,512]{1,0:T(8,128)(2,1)S(1)} collective-permute-done((bf16[256,512]{1,0:T(8,128)(2,1)S(1)}, bf16[256,512]{1,0:T(8,128)(2,1)S(1)}, u32[]{:S(2)}, u32[]{:S(2)}) %collective-permute-start.3) | collective-permute-done | bytes 262176 | tf_op jit(solution)/shard_map/ppermute | solution.py:310
  15.2 1.9 %collective-permute-start.5 = (bf16[256,512]{1,0:T(8,128)(2,1)S(1)}, bf16[256,512]{1,0:T(8,128)(2,1)S(1)}, u32[]{:S(2)}, u32[]{:S(2)}) collective-permute-start(bf16[256,512]{1,0:T(8,128)(2,1)S(1)} %collective-permute-done.3.kv), channel_id=1, source_target_pairs={{0,8},{4,12},{8,16},{12,20},{16,24},{20,28},{24,32},{28,36},{32,40... | collective-permute-start | bytes 786440 | tf_op jit(solution)/shard_map/ppermute | solution.py:340
  17.1 0.0 collective-permute-done.recv
  17.1 3.1 %first.1 = (bf16[512,1024]{1,0:T(8,128)(2,1)S(1)}, f32[512,1024]{1,0:T(8,128)S(1)}, f32[512,1024]{1,0:T(8,128)S(1)}, f32[512,1024]{1,0:T(8,128)S(1)}, f32[8,128]{1,0:T(8,128)S(1)}) custom-call(s32[32]{0:T(128)S(4)} %get-tuple-element.49.meta, s32[512,128]{1,0:T(8,128)S(1)} %get-tuple-element.50.low_key, bf16[256,1024]{1,0:T(8,128)(2,1)S(1)} %get-tuple-element.51.own, ...), custom_call_target="tpu_custom_call" | custom-call | flops 3449999872 | bytes 1048576 | tf_op jit(solution)/shard_map/first/pallas_call | solution.py:325
  20.2 0.5 collective-permute-done.1.buffer_ref
  20.7 1.9 %collective-permute-start.2 = (bf16[256,512]{1,0:T(8,128)(2,1)S(1)}, bf16[256,512]{1,0:T(8,128)(2,1)S(1)}, u32[]{:S(2)}, u32[]{:S(2)}) collective-permute-start(bf16[256,512]{1,0:T(8,128)(2,1)S(1)} %touch.5.kv), channel_id=1, source_target_pairs={{0,8},{4,12},{8,16},{12,20},{16,24},{20,28},{24,32},{28,36},{32,40... | collective-permute-start | bytes 786440 | tf_op jit(solution)/shard_map/ppermute | solution.py:340
  22.6 2.1 %next.7 = (f32[512,1024]{1,0:T(8,128)S(1)}, f32[512,1024]{1,0:T(8,128)S(1)}, f32[512,1024]{1,0:T(8,128)S(1)}, f32[8,128]{1,0:T(8,128)S(1)}) custom-call(s32[32]{0:T(128)S(4)} %get-tuple-element.49.meta, s32[512,128]{1,0:T(8,128)S(1)} %get-tuple-element.50.low_key, ...), custom_call_target="tpu_custom_call", output_to_operand_aliasing={{0}: (4, {}), {1}: (5, {}), {2}: (6, {})} | custom-call | flops 1150000000 | bytes 1048576 | tf_op jit(solution)/shard_map/next/pallas_call | solution.py:375
  24.7 3.2 %collective-permute-done.5.buffer_ref = bf16[256,512]{1,0:T(8,128)(2,1)S(1)} collective-permute-done((bf16[256,512]{1,0:T(8,128)(2,1)S(1)}, bf16[256,512]{1,0:T(8,128)(2,1)S(1)}, u32[]{:S(2)}, u32[]{:S(2)}) %collective-permute-start.5) | collective-permute-done | bytes 262176 | tf_op jit(solution)/shard_map/ppermute | solution.py:340
  27.9 1.9 %collective-permute-start.7 = (bf16[256,512]{1,0:T(8,128)(2,1)S(1)}, bf16[256,512]{1,0:T(8,128)(2,1)S(1)}, u32[]{:S(2)}, u32[]{:S(2)}) collective-permute-start(bf16[256,512]{1,0:T(8,128)(2,1)S(1)} %touch.7.kv), channel_id=1, source_target_pairs={{0,8},{4,12},{8,16},{12,20},{16,24},{20,28},{24,32},{28,36},{32,40... | collective-permute-start | bytes 786440 | tf_op jit(solution)/shard_map/ppermute | solution.py:340
  29.8 2.1 %next.8 = (f32[512,1024]{1,0:T(8,128)S(1)}, f32[512,1024]{1,0:T(8,128)S(1)}, f32[512,1024]{1,0:T(8,128)S(1)}, f32[8,128]{1,0:T(8,128)S(1)}) custom-call(s32[32]{0:T(128)S(4)} %get-tuple-element.49.meta, s32[512,128]{1,0:T(8,128)S(1)} %get-tuple-element.50.low_key, ...), custom_call_target="tpu_custom_call", output_to_operand_aliasing={{0}: (4, {}), {1}: (5, {}), {2}: (6, {})} | custom-call | flops 1150000000 | bytes 1048576 | tf_op jit(solution)/shard_map/next/pallas_call | solution.py:375
  31.9 0.7 %collective-permute-done.2.buffer_ref = bf16[256,512]{1,0:T(8,128)(2,1)S(1)} collective-permute-done((bf16[256,512]{1,0:T(8,128)(2,1)S(1)}, bf16[256,512]{1,0:T(8,128)(2,1)S(1)}, u32[]{:S(2)}, u32[]{:S(2)}) %collective-permute-start.2) | collective-permute-done | bytes 262176 | tf_op jit(solution)/shard_map/ppermute | solution.py:340
  32.6 1.9 %collective-permute-start.4 = (bf16[256,512]{1,0:T(8,128)(2,1)S(1)}, bf16[256,512]{1,0:T(8,128)(2,1)S(1)}, u32[]{:S(2)}, u32[]{:S(2)}) collective-permute-start(bf16[256,512]{1,0:T(8,128)(2,1)S(1)} %touch.6.kv), channel_id=1, source_target_pairs={{0,8},{4,12},{8,16},{12,20},{16,24},{20,28},{24,32},{28,36},{32,40... | collective-permute-start | bytes 786440 | tf_op jit(solution)/shard_map/ppermute | solution.py:340
  34.5 0.1 next.9
  34.6 5.0 %collective-permute-done.7.buffer_ref = bf16[256,512]{1,0:T(8,128)(2,1)S(1)} collective-permute-done((bf16[256,512]{1,0:T(8,128)(2,1)S(1)}, bf16[256,512]{1,0:T(8,128)(2,1)S(1)}, u32[]{:S(2)}, u32[]{:S(2)}) %collective-permute-start.7) | collective-permute-done | bytes 262176 | tf_op jit(solution)/shard_map/ppermute | solution.py:340
  39.6 1.9 %collective-permute-start.8 = (bf16[256,512]{1,0:T(8,128)(2,1)S(1)}, bf16[256,512]{1,0:T(8,128)(2,1)S(1)}, u32[]{:S(2)}, u32[]{:S(2)}) collective-permute-start(bf16[256,512]{1,0:T(8,128)(2,1)S(1)} %touch.9.kv), channel_id=1, source_target_pairs={{0,8},{4,12},{8,16},{12,20},{16,24},{20,28},{24,32},{28,36},{32,40... | collective-permute-start | bytes 786440 | tf_op jit(solution)/shard_map/ppermute | solution.py:340
  41.5 2.2 %next.10 = (f32[512,1024]{1,0:T(8,128)S(1)}, f32[512,1024]{1,0:T(8,128)S(1)}, f32[512,1024]{1,0:T(8,128)S(1)}, f32[8,128]{1,0:T(8,128)S(1)}) custom-call(s32[32]{0:T(128)S(4)} %get-tuple-element.49.meta, s32[512,128]{1,0:T(8,128)S(1)} %get-tuple-element.50.low_key, ...), custom_call_target="tpu_custom_call", output_to_operand_aliasing={{0}: (4, {}), {1}: (5, {}), {2}: (6, {})} | custom-call | flops 1150000000 | bytes 1048576 | tf_op jit(solution)/shard_map/next/pallas_call | solution.py:375
  43.7 1.6 %collective-permute-done.4.buffer_ref = bf16[256,512]{1,0:T(8,128)(2,1)S(1)} collective-permute-done((bf16[256,512]{1,0:T(8,128)(2,1)S(1)}, bf16[256,512]{1,0:T(8,128)(2,1)S(1)}, u32[]{:S(2)}, u32[]{:S(2)}) %collective-permute-start.4) | collective-permute-done | bytes 262176 | tf_op jit(solution)/shard_map/ppermute | solution.py:340
  45.3 2.1 %collective-permute-start.6 = (bf16[256,512]{1,0:T(8,128)(2,1)S(1)}, bf16[256,512]{1,0:T(8,128)(2,1)S(1)}, u32[]{:S(2)}, u32[]{:S(2)}) collective-permute-start(bf16[256,512]{1,0:T(8,128)(2,1)S(1)} %touch.8.kv), channel_id=1, source_target_pairs={{0,8},{4,12},{8,16},{12,20},{16,24},{20,28},{24,32},{28,36},{32,40... | collective-permute-start | bytes 786440 | tf_op jit(solution)/shard_map/ppermute | solution.py:340
  47.4 0.1 next.11
  47.5 0.1 next.12
  47.5 2.5 %collective-permute-done.8.kv = bf16[256,512]{1,0:T(8,128)(2,1)S(1)} collective-permute-done((bf16[256,512]{1,0:T(8,128)(2,1)S(1)}, bf16[256,512]{1,0:T(8,128)(2,1)S(1)}, u32[]{:S(2)}, u32[]{:S(2)}) %collective-permute-start.8) | collective-permute-done | bytes 262176 | tf_op jit(solution)/shard_map/ppermute | solution.py:340
  50.1 7.4 %collective-permute-done.6.kv = bf16[256,512]{1,0:T(8,128)(2,1)S(1)} collective-permute-done((bf16[256,512]{1,0:T(8,128)(2,1)S(1)}, bf16[256,512]{1,0:T(8,128)(2,1)S(1)}, u32[]{:S(2)}, u32[]{:S(2)}) %collective-permute-start.6) | collective-permute-done | bytes 262176 | tf_op jit(solution)/shard_map/ppermute | solution.py:340
  57.4 0.5 last.1
  57.9 4.4 %collective-permute-start.9 = (bf16[256,1024]{1,0:T(8,128)(2,1)S(1)}, bf16[256,1024]{1,0:T(8,128)(2,1)S(1)}, u32[]{:S(2)}, u32[]{:S(2)}) collective-permute-start(bf16[256,1024]{1,0:T(8,128)(2,1)S(1)} %get-tuple-element.84), channel_id=1, source_target_pairs={{0,4},{4,0},{8,12},{12,8},{16,20},{20,16},{24,28},{28,24},{32,36},... | collective-permute-start | bytes 1572872 | tf_op jit(solution)/shard_map/ppermute | solution.py:348
  62.3 1.3 %keep.1.partial = bf16[256,2048]{1,0:T(8,128)(2,1)} custom-call(s32[32]{0:T(128)S(4)} %get-tuple-element.49.meta, f32[512,1024]{1,0:T(8,128)S(1)} %get-tuple-element.85.acc, f32[512,1024]{1,0:T(8,128)S(1)} %get-tuple-element.86.low), custom_call_target="tpu_custom_call" | custom-call | flops 575000000 | bytes 1048576 | tf_op jit(solution)/shard_map/keep/pallas_call | solution.py:349
  63.6 0.2 collective-permute-done.9.got
  63.8 0.8 %join.1 = bf16[256,2048]{1,0:T(8,128)(2,1)} custom-call(bf16[256,1024]{1,0:T(8,128)(2,1)S(1)} %collective-permute-done.9.got, bf16[256,2048]{1,0:T(8,128)(2,1)} %keep.1.partial), custom_call_target="tpu_custom_call", output_to_operand_aliasing={{}: (1, {})} | custom-call | tf_op jit(solution)/shard_map/join/pallas_call | solution.py:359
  (6 shorter events, 0.0 us)
Async XLA Ops:
  1.1 14.1 %collective-permute-start.3 = (bf16[256,512]{1,0:T(8,128)(2,1)S(1)}, bf16[256,512]{1,0:T(8,128)(2,1)S(1)}, u32[]{:S(2)}, u32[]{:S(2)}) collective-permute-start(bf16[256,512]{1,0:T(8,128)(2,1)S(1)} %get-tuple-element.46.cross), channel_id=1, source_target_pairs={{0,12},{4,8},{8,20},{12,16},{16,28},{20,24},{24,36},{28,32},{32,44... | collective-permute-start | bytes 786440 | tf_op jit(solution)/shard_map/ppermute | solution.py:310
  6.2 11.0 %collective-permute-start = (bf16[256,1536]{1,0:T(8,128)(2,1)S(1)}, bf16[256,1536]{1,0:T(8,128)(2,1)S(1)}, u32[]{:S(2)}, u32[]{:S(2)}) collective-permute-start(bf16[256,1536]{1,0:T(8,128)(2,1)S(1)} %get-tuple-element.53), channel_id=1, source_target_pairs={{0,4},{4,0},{8,12},{12,8},{16,20},{20,16},{24,28},{28,24},{32,36},... | collective-permute-start | bytes 2359304 | tf_op jit(solution)/shard_map/ppermute | solution.py:311
  8.1 12.6 %collective-permute-start.1 = (bf16[256,512]{1,0:T(8,128)(2,1)S(1)}, bf16[256,512]{1,0:T(8,128)(2,1)S(1)}, u32[]{:S(2)}, u32[]{:S(2)}) collective-permute-start(bf16[256,512]{1,0:T(8,128)(2,1)S(1)} %get-tuple-element.52.near), channel_id=1, source_target_pairs={{0,8},{4,12},{8,16},{12,20},{16,24},{20,28},{24,32},{28,36},{32,40... | collective-permute-start | bytes 786440 | tf_op jit(solution)/shard_map/ppermute | solution.py:310
  15.2 12.7 %collective-permute-start.5 = (bf16[256,512]{1,0:T(8,128)(2,1)S(1)}, bf16[256,512]{1,0:T(8,128)(2,1)S(1)}, u32[]{:S(2)}, u32[]{:S(2)}) collective-permute-start(bf16[256,512]{1,0:T(8,128)(2,1)S(1)} %collective-permute-done.3.kv), channel_id=1, source_target_pairs={{0,8},{4,12},{8,16},{12,20},{16,24},{20,28},{24,32},{28,36},{32,40... | collective-permute-start | bytes 786440 | tf_op jit(solution)/shard_map/ppermute | solution.py:340
  20.7 11.9 %collective-permute-start.2 = (bf16[256,512]{1,0:T(8,128)(2,1)S(1)}, bf16[256,512]{1,0:T(8,128)(2,1)S(1)}, u32[]{:S(2)}, u32[]{:S(2)}) collective-permute-start(bf16[256,512]{1,0:T(8,128)(2,1)S(1)} %touch.5.kv), channel_id=1, source_target_pairs={{0,8},{4,12},{8,16},{12,20},{16,24},{20,28},{24,32},{28,36},{32,40... | collective-permute-start | bytes 786440 | tf_op jit(solution)/shard_map/ppermute | solution.py:340
  27.9 11.7 %collective-permute-start.7 = (bf16[256,512]{1,0:T(8,128)(2,1)S(1)}, bf16[256,512]{1,0:T(8,128)(2,1)S(1)}, u32[]{:S(2)}, u32[]{:S(2)}) collective-permute-start(bf16[256,512]{1,0:T(8,128)(2,1)S(1)} %touch.7.kv), channel_id=1, source_target_pairs={{0,8},{4,12},{8,16},{12,20},{16,24},{20,28},{24,32},{28,36},{32,40... | collective-permute-start | bytes 786440 | tf_op jit(solution)/shard_map/ppermute | solution.py:340
  32.6 12.7 %collective-permute-start.4 = (bf16[256,512]{1,0:T(8,128)(2,1)S(1)}, bf16[256,512]{1,0:T(8,128)(2,1)S(1)}, u32[]{:S(2)}, u32[]{:S(2)}) collective-permute-start(bf16[256,512]{1,0:T(8,128)(2,1)S(1)} %touch.6.kv), channel_id=1, source_target_pairs={{0,8},{4,12},{8,16},{12,20},{16,24},{20,28},{24,32},{28,36},{32,40... | collective-permute-start | bytes 786440 | tf_op jit(solution)/shard_map/ppermute | solution.py:340
  39.6 10.4 %collective-permute-start.8 = (bf16[256,512]{1,0:T(8,128)(2,1)S(1)}, bf16[256,512]{1,0:T(8,128)(2,1)S(1)}, u32[]{:S(2)}, u32[]{:S(2)}) collective-permute-start(bf16[256,512]{1,0:T(8,128)(2,1)S(1)} %touch.9.kv), channel_id=1, source_target_pairs={{0,8},{4,12},{8,16},{12,20},{16,24},{20,28},{24,32},{28,36},{32,40... | collective-permute-start | bytes 786440 | tf_op jit(solution)/shard_map/ppermute | solution.py:340
  45.3 12.1 %collective-permute-start.6 = (bf16[256,512]{1,0:T(8,128)(2,1)S(1)}, bf16[256,512]{1,0:T(8,128)(2,1)S(1)}, u32[]{:S(2)}, u32[]{:S(2)}) collective-permute-start(bf16[256,512]{1,0:T(8,128)(2,1)S(1)} %touch.8.kv), channel_id=1, source_target_pairs={{0,8},{4,12},{8,16},{12,20},{16,24},{20,28},{24,32},{28,36},{32,40... | collective-permute-start | bytes 786440 | tf_op jit(solution)/shard_map/ppermute | solution.py:340
  57.9 5.9 %collective-permute-start.9 = (bf16[256,1024]{1,0:T(8,128)(2,1)S(1)}, bf16[256,1024]{1,0:T(8,128)(2,1)S(1)}, u32[]{:S(2)}, u32[]{:S(2)}) collective-permute-start(bf16[256,1024]{1,0:T(8,128)(2,1)S(1)} %get-tuple-element.84), channel_id=1, source_target_pairs={{0,4},{4,0},{8,12},{12,8},{16,20},{20,16},{24,28},{28,24},{32,36},... | collective-permute-start | bytes 1572872 | tf_op jit(solution)/shard_map/ppermute | solution.py:348

commit v3 on v2

--- a/solution.py
+++ b/solution.py
@@ -335,7 +335,7 @@
     tokens = [None, token]
     for index in range(6):
         kv = arrived[index]
-        if index:
+        if index > 1:
             kv = arrived[index] = touch(kv, tokens[index])
         arrived.append(shift(kv, perm=same))
         if index == 0:

time: 65.1 us -> 65.2 us (level)
  the two profiles are of different devices: /device:TPU:257 before, /device:TPU:263 now
where the time goes in v3:
time: 65.2 us; the launch traced here: 64.8 us
  waiting for transfers between devices  27.7 us (42%)
  starting transfers between devices  24.9 us (38%)
  Pallas kernels  11.9 us (18%)
    ppermute x6, waiting for transfers between devices, local(): arrived.append(shift(kv, perm=same))  20.3 us
    ppermute x6, starting transfers between devices, local(): arrived.append(shift(kv, perm=same))  11.6 us
    ppermute x2, waiting for transfers between devices, local(): arrived = [shift(cross, perm=other), shift(near, perm=same)]  7.16 us
    ppermute x2, starting transfers between devices, local(): arrived = [shift(cross, perm=other), shift(near, perm=same)]  6.97 us
    ppermute x1, starting transfers between devices, local(): got = shift(send, perm=pair)  4.34 us
    pallas_call x8, Pallas kernels, step(): pl.pallas_call(functools.partial(kernel, index // 2 + 1, 1 - index % 2),...  3.96 us
    pallas_call x1, Pallas kernels, local(): pl.pallas_call(first_kernel, out_shape=[pltpu.VMEM((2 * ROWS, HALF), bf16...  3.11 us
    ppermute x1, starting transfers between devices, local(): recv = fast(shift(swap, perm=pair))  1.92 us
  transfers between devices with their start and end apart: 10, of which 9 were waited for; matrix products, arithmetic and copies ran while one was open for 0% of the time, Pallas kernels for 15%

profile of v3, /device:TPU:263, one launch (start us, length us, event | category | flops | bytes accessed | tf_op | source)
XLA Modules:
  0.0 64.8 jit_solution(8589430513049012836)
XLA Ops:
  0.0 1.1 %near.1 = (bf16[256,512]{1,0:T(8,128)(2,1)S(1)}, bf16[256,512]{1,0:T(8,128)(2,1)S(1)}) custom-call(bf16[256,512]{1,0:T(8,128)(2,1)} %k.1, bf16[256,512]{1,0:T(8,128)(2,1)} %v.1), custom_call_target="tpu_custom_call" | custom-call | tf_op jit(solution)/shard_map/near/pallas_call | solution.py:281
  1.1 3.8 %collective-permute-start.3 = (bf16[256,512]{1,0:T(8,128)(2,1)S(1)}, bf16[256,512]{1,0:T(8,128)(2,1)S(1)}, u32[]{:S(2)}, u32[]{:S(2)}) collective-permute-start(bf16[256,512]{1,0:T(8,128)(2,1)S(1)} %get-tuple-element.45.cross), channel_id=1, source_target_pairs={{0,12},{4,8},{8,20},{12,16},{16,28},{20,24},{24,36},{28,32},{32,44... | collective-permute-start | bytes 786440 | tf_op jit(solution)/shard_map/ppermute | solution.py:310
  4.9 1.3 %pack.1 = (bf16[256,1536]{1,0:T(8,128)(2,1)S(1)}, bf16[256,1024]{1,0:T(8,128)(2,1)S(1)}, s32[1,128]{1,0:T(1,128)S(1)}, s32[256]{0:T(256)S(4)}) custom-call(bf16[256,2048]{1,0:T(8,128)(2,1)} %q.1, bf16[256,512]{1,0:T(8,128)(2,1)S(1)} %get-tuple-element.45.cross, s32[1,128]{1,0:T(1,128)} %bitcast.1, s32[256]{0:T(256)} %home.1), custom_call_target="tpu_custom_call" | custom-call | tf_op jit(solution)/shard_map/pack/pallas_call | solution.py:291
  6.2 1.9 %collective-permute-start = (bf16[256,1536]{1,0:T(8,128)(2,1)S(1)}, bf16[256,1536]{1,0:T(8,128)(2,1)S(1)}, u32[]{:S(2)}, u32[]{:S(2)}) collective-permute-start(bf16[256,1536]{1,0:T(8,128)(2,1)S(1)} %get-tuple-element.52), channel_id=1, source_target_pairs={{0,4},{4,0},{8,12},{12,8},{16,20},{20,16},{24,28},{28,24},{32,36},... | collective-permute-start | bytes 2359304 | tf_op jit(solution)/shard_map/ppermute | solution.py:311
  8.1 3.2 %collective-permute-start.1 = (bf16[256,512]{1,0:T(8,128)(2,1)S(1)}, bf16[256,512]{1,0:T(8,128)(2,1)S(1)}, u32[]{:S(2)}, u32[]{:S(2)}) collective-permute-start(bf16[256,512]{1,0:T(8,128)(2,1)S(1)} %get-tuple-element.51.near), channel_id=1, source_target_pairs={{0,8},{4,12},{8,16},{12,20},{16,24},{20,28},{24,32},{28,36},{32,40... | collective-permute-start | bytes 786440 | tf_op jit(solution)/shard_map/ppermute | solution.py:310
  11.3 0.3 plan.1
  11.6 3.6 %collective-permute-done.3.kv = bf16[256,512]{1,0:T(8,128)(2,1)S(1)} collective-permute-done((bf16[256,512]{1,0:T(8,128)(2,1)S(1)}, bf16[256,512]{1,0:T(8,128)(2,1)S(1)}, u32[]{:S(2)}, u32[]{:S(2)}) %collective-permute-start.3) | collective-permute-done | bytes 262176 | tf_op jit(solution)/shard_map/ppermute | solution.py:310
  15.2 1.9 %collective-permute-start.5 = (bf16[256,512]{1,0:T(8,128)(2,1)S(1)}, bf16[256,512]{1,0:T(8,128)(2,1)S(1)}, u32[]{:S(2)}, u32[]{:S(2)}) collective-permute-start(bf16[256,512]{1,0:T(8,128)(2,1)S(1)} %collective-permute-done.3.kv), channel_id=1, source_target_pairs={{0,8},{4,12},{8,16},{12,20},{16,24},{20,28},{24,32},{28,36},{32,40... | collective-permute-start | bytes 786440 | tf_op jit(solution)/shard_map/ppermute | solution.py:340
  17.1 3.6 %collective-permute-done.1.kv = bf16[256,512]{1,0:T(8,128)(2,1)S(1)} collective-permute-done((bf16[256,512]{1,0:T(8,128)(2,1)S(1)}, bf16[256,512]{1,0:T(8,128)(2,1)S(1)}, u32[]{:S(2)}, u32[]{:S(2)}) %collective-permute-start.1) | collective-permute-done | bytes 262176 | tf_op jit(solution)/shard_map/ppermute | solution.py:310
  20.7 1.9 %collective-permute-start.2 = (bf16[256,512]{1,0:T(8,128)(2,1)S(1)}, bf16[256,512]{1,0:T(8,128)(2,1)S(1)}, u32[]{:S(2)}, u32[]{:S(2)}) collective-permute-start(bf16[256,512]{1,0:T(8,128)(2,1)S(1)} %collective-permute-done.1.kv), channel_id=1, source_target_pairs={{0,8},{4,12},{8,16},{12,20},{16,24},{20,28},{24,32},{28,36},{32,40... | collective-permute-start | bytes 786440 | tf_op jit(solution)/shard_map/ppermute | solution.py:340
  22.6 0.0 collective-permute-done.recv
  22.6 3.1 %first.1 = (bf16[512,1024]{1,0:T(8,128)(2,1)S(1)}, f32[512,1024]{1,0:T(8,128)S(1)}, f32[512,1024]{1,0:T(8,128)S(1)}, f32[512,1024]{1,0:T(8,128)S(1)}, f32[8,128]{1,0:T(8,128)}) custom-call(s32[32]{0:T(128)S(4)} %get-tuple-element.48.meta, s32[512,128]{1,0:T(8,128)S(1)} %get-tuple-element.49.low_key, bf16[256,1024]{1,0:T(8,128)(2,1)S(1)} %get-tuple-element.50.own, ...), custom_call_target="tpu_custom_call" | custom-call | flops 3449999872 | bytes 1048576 | tf_op jit(solution)/shard_map/first/pallas_call | solution.py:325
  25.7 1.1 %next.7 = (f32[512,1024]{1,0:T(8,128)S(1)}, f32[512,1024]{1,0:T(8,128)S(1)}, f32[512,1024]{1,0:T(8,128)S(1)}, f32[8,128]{1,0:T(8,128)S(1)}) custom-call(s32[32]{0:T(128)S(4)} %get-tuple-element.48.meta, s32[512,128]{1,0:T(8,128)S(1)} %get-tuple-element.49.low_key, ...), custom_call_target="tpu_custom_call", output_to_operand_aliasing={{0}: (4, {}), {1}: (5, {}), {2}: (6, {})} | custom-call | flops 1150000000 | bytes 1048576 | tf_op jit(solution)/shard_map/next/pallas_call | solution.py:375
  26.9 1.0 %collective-permute-done.5.buffer_ref = bf16[256,512]{1,0:T(8,128)(2,1)S(1)} collective-permute-done((bf16[256,512]{1,0:T(8,128)(2,1)S(1)}, bf16[256,512]{1,0:T(8,128)(2,1)S(1)}, u32[]{:S(2)}, u32[]{:S(2)}) %collective-permute-start.5) | collective-permute-done | bytes 262176 | tf_op jit(solution)/shard_map/ppermute | solution.py:340
  27.9 1.9 %collective-permute-start.7 = (bf16[256,512]{1,0:T(8,128)(2,1)S(1)}, bf16[256,512]{1,0:T(8,128)(2,1)S(1)}, u32[]{:S(2)}, u32[]{:S(2)}) collective-permute-start(bf16[256,512]{1,0:T(8,128)(2,1)S(1)} %touch.5.kv), channel_id=1, source_target_pairs={{0,8},{4,12},{8,16},{12,20},{16,24},{20,28},{24,32},{28,36},{32,40... | collective-permute-start | bytes 786440 | tf_op jit(solution)/shard_map/ppermute | solution.py:340
  29.8 1.1 %next.8 = (f32[512,1024]{1,0:T(8,128)S(1)}, f32[512,1024]{1,0:T(8,128)S(1)}, f32[512,1024]{1,0:T(8,128)S(1)}, f32[8,128]{1,0:T(8,128)S(1)}) custom-call(s32[32]{0:T(128)S(4)} %get-tuple-element.48.meta, s32[512,128]{1,0:T(8,128)S(1)} %get-tuple-element.49.low_key, ...), custom_call_target="tpu_custom_call", output_to_operand_aliasing={{0}: (4, {}), {1}: (5, {}), {2}: (6, {})} | custom-call | flops 1150000000 | bytes 1048576 | tf_op jit(solution)/shard_map/next/pallas_call | solution.py:375
  31.0 1.7 %collective-permute-done.2.buffer_ref = bf16[256,512]{1,0:T(8,128)(2,1)S(1)} collective-permute-done((bf16[256,512]{1,0:T(8,128)(2,1)S(1)}, bf16[256,512]{1,0:T(8,128)(2,1)S(1)}, u32[]{:S(2)}, u32[]{:S(2)}) %collective-permute-start.2) | collective-permute-done | bytes 262176 | tf_op jit(solution)/shard_map/ppermute | solution.py:340
  32.6 1.9 %collective-permute-start.4 = (bf16[256,512]{1,0:T(8,128)(2,1)S(1)}, bf16[256,512]{1,0:T(8,128)(2,1)S(1)}, u32[]{:S(2)}, u32[]{:S(2)}) collective-permute-start(bf16[256,512]{1,0:T(8,128)(2,1)S(1)} %touch.4.kv), channel_id=1, source_target_pairs={{0,8},{4,12},{8,16},{12,20},{16,24},{20,28},{24,32},{28,36},{32,40... | collective-permute-start | bytes 786440 | tf_op jit(solution)/shard_map/ppermute | solution.py:340
  34.5 0.1 next.9
  34.6 5.0 %collective-permute-done.7.buffer_ref = bf16[256,512]{1,0:T(8,128)(2,1)S(1)} collective-permute-done((bf16[256,512]{1,0:T(8,128)(2,1)S(1)}, bf16[256,512]{1,0:T(8,128)(2,1)S(1)}, u32[]{:S(2)}, u32[]{:S(2)}) %collective-permute-start.7) | collective-permute-done | bytes 262176 | tf_op jit(solution)/shard_map/ppermute | solution.py:340
  39.6 1.9 %collective-permute-start.8 = (bf16[256,512]{1,0:T(8,128)(2,1)S(1)}, bf16[256,512]{1,0:T(8,128)(2,1)S(1)}, u32[]{:S(2)}, u32[]{:S(2)}) collective-permute-start(bf16[256,512]{1,0:T(8,128)(2,1)S(1)} %touch.7.kv), channel_id=1, source_target_pairs={{0,8},{4,12},{8,16},{12,20},{16,24},{20,28},{24,32},{28,36},{32,40... | collective-permute-start | bytes 786440 | tf_op jit(solution)/shard_map/ppermute | solution.py:340
  41.5 1.1 %next.10 = (f32[512,1024]{1,0:T(8,128)S(1)}, f32[512,1024]{1,0:T(8,128)S(1)}, f32[512,1024]{1,0:T(8,128)S(1)}, f32[8,128]{1,0:T(8,128)S(1)}) custom-call(s32[32]{0:T(128)S(4)} %get-tuple-element.48.meta, s32[512,128]{1,0:T(8,128)S(1)} %get-tuple-element.49.low_key, ...), custom_call_target="tpu_custom_call", output_to_operand_aliasing={{0}: (4, {}), {1}: (5, {}), {2}: (6, {})} | custom-call | flops 1150000000 | bytes 1048576 | tf_op jit(solution)/shard_map/next/pallas_call | solution.py:375
  42.6 2.7 %collective-permute-done.4.buffer_ref = bf16[256,512]{1,0:T(8,128)(2,1)S(1)} collective-permute-done((bf16[256,512]{1,0:T(8,128)(2,1)S(1)}, bf16[256,512]{1,0:T(8,128)(2,1)S(1)}, u32[]{:S(2)}, u32[]{:S(2)}) %collective-permute-start.4) | collective-permute-done | bytes 262176 | tf_op jit(solution)/shard_map/ppermute | solution.py:340
  45.3 2.1 %collective-permute-start.6 = (bf16[256,512]{1,0:T(8,128)(2,1)S(1)}, bf16[256,512]{1,0:T(8,128)(2,1)S(1)}, u32[]{:S(2)}, u32[]{:S(2)}) collective-permute-start(bf16[256,512]{1,0:T(8,128)(2,1)S(1)} %touch.6.kv), channel_id=1, source_target_pairs={{0,8},{4,12},{8,16},{12,20},{16,24},{20,28},{24,32},{28,36},{32,40... | collective-permute-start | bytes 786440 | tf_op jit(solution)/shard_map/ppermute | solution.py:340
  47.4 0.1 next.11
  47.5 0.1 next.12
  47.5 2.5 %collective-permute-done.8.kv = bf16[256,512]{1,0:T(8,128)(2,1)S(1)} collective-permute-done((bf16[256,512]{1,0:T(8,128)(2,1)S(1)}, bf16[256,512]{1,0:T(8,128)(2,1)S(1)}, u32[]{:S(2)}, u32[]{:S(2)}) %collective-permute-start.8) | collective-permute-done | bytes 262176 | tf_op jit(solution)/shard_map/ppermute | solution.py:340
  50.0 7.5 %collective-permute-done.6.kv = bf16[256,512]{1,0:T(8,128)(2,1)S(1)} collective-permute-done((bf16[256,512]{1,0:T(8,128)(2,1)S(1)}, bf16[256,512]{1,0:T(8,128)(2,1)S(1)}, u32[]{:S(2)}, u32[]{:S(2)}) %collective-permute-start.6) | collective-permute-done | bytes 262176 | tf_op jit(solution)/shard_map/ppermute | solution.py:340
  57.4 0.5 last.1
  57.9 4.3 %collective-permute-start.9 = (bf16[256,1024]{1,0:T(8,128)(2,1)S(1)}, bf16[256,1024]{1,0:T(8,128)(2,1)S(1)}, u32[]{:S(2)}, u32[]{:S(2)}) collective-permute-start(bf16[256,1024]{1,0:T(8,128)(2,1)S(1)} %get-tuple-element.82), channel_id=1, source_target_pairs={{0,4},{4,0},{8,12},{12,8},{16,20},{20,16},{24,28},{28,24},{32,36},... | collective-permute-start | bytes 1572872 | tf_op jit(solution)/shard_map/ppermute | solution.py:348
  62.3 1.3 %keep.1.partial = bf16[256,2048]{1,0:T(8,128)(2,1)} custom-call(s32[32]{0:T(128)S(4)} %get-tuple-element.48.meta, f32[512,1024]{1,0:T(8,128)S(1)} %get-tuple-element.83.acc, f32[512,1024]{1,0:T(8,128)S(1)} %get-tuple-element.84.low), custom_call_target="tpu_custom_call" | custom-call | flops 575000000 | bytes 1048576 | tf_op jit(solution)/shard_map/keep/pallas_call | solution.py:349
  63.6 0.2 collective-permute-done.9.got
  63.8 0.8 %join.1 = bf16[256,2048]{1,0:T(8,128)(2,1)} custom-call(bf16[256,1024]{1,0:T(8,128)(2,1)S(1)} %collective-permute-done.9.got, bf16[256,2048]{1,0:T(8,128)(2,1)} %keep.1.partial), custom_call_target="tpu_custom_call", output_to_operand_aliasing={{}: (1, {})} | custom-call | tf_op jit(solution)/shard_map/join/pallas_call | solution.py:359
  (5 shorter events, 0.0 us)
Async XLA Ops:
  1.1 14.1 %collective-permute-start.3 = (bf16[256,512]{1,0:T(8,128)(2,1)S(1)}, bf16[256,512]{1,0:T(8,128)(2,1)S(1)}, u32[]{:S(2)}, u32[]{:S(2)}) collective-permute-start(bf16[256,512]{1,0:T(8,128)(2,1)S(1)} %get-tuple-element.45.cross), channel_id=1, source_target_pairs={{0,12},{4,8},{8,20},{12,16},{16,28},{20,24},{24,36},{28,32},{32,44... | collective-permute-start | bytes 786440 | tf_op jit(solution)/shard_map/ppermute | solution.py:310
  6.2 16.4 %collective-permute-start = (bf16[256,1536]{1,0:T(8,128)(2,1)S(1)}, bf16[256,1536]{1,0:T(8,128)(2,1)S(1)}, u32[]{:S(2)}, u32[]{:S(2)}) collective-permute-start(bf16[256,1536]{1,0:T(8,128)(2,1)S(1)} %get-tuple-element.52), channel_id=1, source_target_pairs={{0,4},{4,0},{8,12},{12,8},{16,20},{20,16},{24,28},{28,24},{32,36},... | collective-permute-start | bytes 2359304 | tf_op jit(solution)/shard_map/ppermute | solution.py:311
  8.1 12.6 %collective-permute-start.1 = (bf16[256,512]{1,0:T(8,128)(2,1)S(1)}, bf16[256,512]{1,0:T(8,128)(2,1)S(1)}, u32[]{:S(2)}, u32[]{:S(2)}) collective-permute-start(bf16[256,512]{1,0:T(8,128)(2,1)S(1)} %get-tuple-element.51.near), channel_id=1, source_target_pairs={{0,8},{4,12},{8,16},{12,20},{16,24},{20,28},{24,32},{28,36},{32,40... | collective-permute-start | bytes 786440 | tf_op jit(solution)/shard_map/ppermute | solution.py:310
  15.2 12.7 %collective-permute-start.5 = (bf16[256,512]{1,0:T(8,128)(2,1)S(1)}, bf16[256,512]{1,0:T(8,128)(2,1)S(1)}, u32[]{:S(2)}, u32[]{:S(2)}) collective-permute-start(bf16[256,512]{1,0:T(8,128)(2,1)S(1)} %collective-permute-done.3.kv), channel_id=1, source_target_pairs={{0,8},{4,12},{8,16},{12,20},{16,24},{20,28},{24,32},{28,36},{32,40... | collective-permute-start | bytes 786440 | tf_op jit(solution)/shard_map/ppermute | solution.py:340
  20.7 11.9 %collective-permute-start.2 = (bf16[256,512]{1,0:T(8,128)(2,1)S(1)}, bf16[256,512]{1,0:T(8,128)(2,1)S(1)}, u32[]{:S(2)}, u32[]{:S(2)}) collective-permute-start(bf16[256,512]{1,0:T(8,128)(2,1)S(1)} %collective-permute-done.1.kv), channel_id=1, source_target_pairs={{0,8},{4,12},{8,16},{12,20},{16,24},{20,28},{24,32},{28,36},{32,40... | collective-permute-start | bytes 786440 | tf_op jit(solution)/shard_map/ppermute | solution.py:340
  27.9 11.6 %collective-permute-start.7 = (bf16[256,512]{1,0:T(8,128)(2,1)S(1)}, bf16[256,512]{1,0:T(8,128)(2,1)S(1)}, u32[]{:S(2)}, u32[]{:S(2)}) collective-permute-start(bf16[256,512]{1,0:T(8,128)(2,1)S(1)} %touch.5.kv), channel_id=1, source_target_pairs={{0,8},{4,12},{8,16},{12,20},{16,24},{20,28},{24,32},{28,36},{32,40... | collective-permute-start | bytes 786440 | tf_op jit(solution)/shard_map/ppermute | solution.py:340
  32.6 12.7 %collective-permute-start.4 = (bf16[256,512]{1,0:T(8,128)(2,1)S(1)}, bf16[256,512]{1,0:T(8,128)(2,1)S(1)}, u32[]{:S(2)}, u32[]{:S(2)}) collective-permute-start(bf16[256,512]{1,0:T(8,128)(2,1)S(1)} %touch.4.kv), channel_id=1, source_target_pairs={{0,8},{4,12},{8,16},{12,20},{16,24},{20,28},{24,32},{28,36},{32,40... | collective-permute-start | bytes 786440 | tf_op jit(solution)/shard_map/ppermute | solution.py:340
  39.6 10.4 %collective-permute-start.8 = (bf16[256,512]{1,0:T(8,128)(2,1)S(1)}, bf16[256,512]{1,0:T(8,128)(2,1)S(1)}, u32[]{:S(2)}, u32[]{:S(2)}) collective-permute-start(bf16[256,512]{1,0:T(8,128)(2,1)S(1)} %touch.7.kv), channel_id=1, source_target_pairs={{0,8},{4,12},{8,16},{12,20},{16,24},{20,28},{24,32},{28,36},{32,40... | collective-permute-start | bytes 786440 | tf_op jit(solution)/shard_map/ppermute | solution.py:340
  45.3 12.1 %collective-permute-start.6 = (bf16[256,512]{1,0:T(8,128)(2,1)S(1)}, bf16[256,512]{1,0:T(8,128)(2,1)S(1)}, u32[]{:S(2)}, u32[]{:S(2)}) collective-permute-start(bf16[256,512]{1,0:T(8,128)(2,1)S(1)} %touch.6.kv), channel_id=1, source_target_pairs={{0,8},{4,12},{8,16},{12,20},{16,24},{20,28},{24,32},{28,36},{32,40... | collective-permute-start | bytes 786440 | tf_op jit(solution)/shard_map/ppermute | solution.py:340
  57.9 5.9 %collective-permute-start.9 = (bf16[256,1024]{1,0:T(8,128)(2,1)S(1)}, bf16[256,1024]{1,0:T(8,128)(2,1)S(1)}, u32[]{:S(2)}, u32[]{:S(2)}) collective-permute-start(bf16[256,1024]{1,0:T(8,128)(2,1)S(1)} %get-tuple-element.82), channel_id=1, source_target_pairs={{0,4},{4,0},{8,12},{12,8},{16,20},{20,16},{24,28},{28,24},{32,36},... | collective-permute-start | bytes 1572872 | tf_op jit(solution)/shard_map/ppermute | solution.py:348
